TPU v7x, 32 devices: a whole 2x2x4 slice. The times are simulated.
32 devices in a mesh: dp: 16 (over z, x, core), tensor: 2 (over y).
Axes of the slice: x: 2, y: 2, z: 4, core: 2. Of those that a mesh axis runs over, the one named last changes fastest.
Arguments:
- inputs: bfloat16 [32768, 512], P('dp'), may hold values from -6 to 6
- memory: bfloat16 [32768, 512], P('dp'), may hold values from -6 to 6
- tgt_seg: int32 [32, 1024], P('dp'), may hold values from 0 to 31, as said below
- src_seg: int32 [32, 1024], P('dp'), may hold values from 0 to 31, as said below
- self_query: bfloat16 [512, 512], P(None, 'tensor'), may hold values from -0.25 to 0.25
- self_key: bfloat16 [512, 512], P(None, 'tensor'), may hold values from -0.25 to 0.25
- self_value: bfloat16 [512, 512], P(None, 'tensor'), may hold values from -0.25 to 0.25
- self_out: bfloat16 [512, 512], P('tensor'), may hold values from -1 to 1
- cross_query: bfloat16 [512, 512], P(None, 'tensor'), may hold values from -0.25 to 0.25
- cross_key: bfloat16 [512, 512], P(None, 'tensor'), may hold values from -0.25 to 0.25
- cross_value: bfloat16 [512, 512], P(None, 'tensor'), may hold values from -0.25 to 0.25
- cross_out: bfloat16 [512, 512], P('tensor'), may hold values from -1 to 1
- ffn_in: bfloat16 [512, 2048], P(None, 'tensor'), may hold values from -0.25 to 0.25
- ffn_out: bfloat16 [2048, 512], P('tensor'), may hold values from -0.125 to 0.125
- norm_gain: float32 [3, 512], replicated, may hold values from 0.25 to 1.75
- norm_shift: float32 [3, 512], replicated, may hold values from -3 to 3
- residual_scale: float32 [3, 512], replicated, may hold values from 0.8 to 2
- cotangent: bfloat16 [32768, 512], P('dp')
Outputs:
- output: bfloat16 [32768, 512], P('dp')
- input_grad: float32 [32768, 512], P('dp', 'tensor')
- memory_grad: float32 [32768, 512], P('dp', 'tensor')
- self_query_grad: float32 [512, 512], P('dp', 'tensor')
- self_key_grad: float32 [512, 512], P('dp', 'tensor')
- self_value_grad: float32 [512, 512], P('dp', 'tensor')
- self_out_grad: float32 [512, 512], P('tensor', 'dp')
- cross_query_grad: float32 [512, 512], P('dp', 'tensor')
- cross_key_grad: float32 [512, 512], P('dp', 'tensor')
- cross_value_grad: float32 [512, 512], P('dp', 'tensor')
- cross_out_grad: float32 [512, 512], P('tensor', 'dp')
- ffn_in_grad: float32 [512, 2048], P('dp', 'tensor')
- ffn_out_grad: float32 [2048, 512], P('tensor', 'dp')
- norm_gain_grad: float32 [3, 512], P(None, 'dp')
- norm_shift_grad: float32 [3, 512], P(None, 'dp')
- residual_scale_grad: float32 [3, 512], P(None, 'dp')
Inputs may be any that keep to these rules, and one draw needn't show every extreme that they name: `tgt_seg`: along each row the ids never fall, and every id from 0 to 31 holds one or more positions of every row; target id s of row r is the same sentence pair as memory id s of row r. `src_seg`: along each row the ids never fall, and every id from 0 to 31 holds one or more positions of every row.
All inputs are finite; a program needn't handle non-finite values.
Results may differ from a plain program's by a relative error of at most 0.025.
Values may be sent and summed in bfloat16 or wider, within the bound.
No kernel may reach another device: no remote copies, remote signals or barrier semaphores. Data moves between devices by JAX's collectives and lax.ppermute only.
A program may use at most 192 MiB of HBM per device.

v0:
```python
import jax
import jax.numpy as jnp
from jax import lax
from jax.sharding import PartitionSpec as P

HEAD_DIM = 64
QBLOCK = 512


def layer_norm(stream, gain, shift):
    center = jnp.mean(stream, axis=-1, keepdims=True)
    centered = stream - center
    variance = jnp.mean(centered * centered, axis=-1, keepdims=True)
    return centered * lax.rsqrt(variance + 1e-05) * gain + shift


def gelu_tanh(value):
    return (
        0.5
        * value
        * (1.0 + jnp.tanh(0.7978845608028654 * (value + 0.044715 * value * value * value)))
    )


def project(left, right):
    return jnp.dot(left, right, preferred_element_type=jnp.float32).astype(jnp.bfloat16)


def contract_rows(left, right):
    return lax.dot_general(
        left, right, (((0,), (0,)), ((), ())), preferred_element_type=jnp.float32
    )


def times_rows(left, right):
    return lax.dot_general(
        left, right, (((1,), (1,)), ((), ())), preferred_element_type=jnp.float32
    )


def branch_total(mixed, weight):
    return lax.psum(
        jnp.dot(mixed, weight, preferred_element_type=jnp.float32).astype(jnp.bfloat16), "tensor"
    ).astype(jnp.float32)


def stream_total(grad, weight):
    return lax.psum(times_rows(grad, weight).astype(jnp.bfloat16), "tensor").astype(jnp.float32)


def block_mask(query_seg, key_seg, first, count, causal):
    allowed = query_seg[first : first + count, None] == key_seg[None, :]
    if causal:
        later = jnp.arange(key_seg.shape[0])[None, :] <= (first + jnp.arange(count))[:, None]
        allowed = allowed & later
    return allowed


def block_scores(query, keys, first, count, allowed):
    scale = float(query.shape[-1]) ** (-0.5)
    scores = (
        jnp.einsum(
            "qhd,khd->hqk", query[first : first + count], keys, preferred_element_type=jnp.float32
        )
        * scale
    )
    return jnp.where(allowed[None], scores, -1e30)


def forward_row(query, keys, values, query_seg, key_seg, causal):
    length = query.shape[0]
    block = min(QBLOCK, length)
    outputs = []
    logs = []
    for first in range(0, length, block):
        scores = block_scores(
            query, keys, first, block, block_mask(query_seg, key_seg, first, block, causal)
        )
        peak = jnp.max(scores, axis=-1, keepdims=True)
        weights = jnp.exp(scores - peak)
        total = jnp.sum(weights, axis=-1, keepdims=True)
        probs = (weights / total).astype(jnp.bfloat16)
        mixed = jnp.einsum("hqk,khd->qhd", probs, values, preferred_element_type=jnp.float32)
        outputs.append(mixed.astype(jnp.bfloat16))
        logs.append((peak + jnp.log(total))[:, :, 0])
    return (jnp.concatenate(outputs, axis=0), jnp.concatenate(logs, axis=1))


def backward_row(query, keys, values, query_seg, key_seg, logsum, d_mixed, causal):
    length = query.shape[0]
    block = min(QBLOCK, length)
    scale = float(query.shape[-1]) ** (-0.5)
    key_grad = jnp.zeros(keys.shape, jnp.float32)
    value_grad = jnp.zeros(values.shape, jnp.float32)
    query_parts = []
    for first in range(0, length, block):
        scores = block_scores(
            query, keys, first, block, block_mask(query_seg, key_seg, first, block, causal)
        )
        probs = jnp.exp(scores - logsum[:, first : first + block, None])
        d_rows = d_mixed[first : first + block]
        d_probs = jnp.einsum("qhd,khd->hqk", d_rows, values, preferred_element_type=jnp.float32)
        centre = jnp.sum(probs * d_probs, axis=-1, keepdims=True)
        d_scores = (probs * (d_probs - centre)).astype(jnp.bfloat16)
        query_parts.append(
            (
                jnp.einsum("hqk,khd->qhd", d_scores, keys, preferred_element_type=jnp.float32)
                * scale
            ).astype(jnp.bfloat16)
        )
        key_grad = (
            key_grad
            + jnp.einsum(
                "hqk,qhd->khd",
                d_scores,
                query[first : first + block],
                preferred_element_type=jnp.float32,
            )
            * scale
        )
        value_grad = value_grad + jnp.einsum(
            "hqk,qhd->khd", probs.astype(jnp.bfloat16), d_rows, preferred_element_type=jnp.float32
        )
    return (
        jnp.concatenate(query_parts, axis=0),
        key_grad.astype(jnp.bfloat16),
        value_grad.astype(jnp.bfloat16),
    )


def split_heads(flat, rows):
    return flat.reshape(rows, flat.shape[0] // rows, flat.shape[1] // HEAD_DIM, HEAD_DIM)


def attend_rows(query, keys, values, query_seg, key_seg, causal):
    rows = query_seg.shape[0]

    def one_row(pack):
        return forward_row(pack[0], pack[1], pack[2], pack[3], pack[4], causal)

    mixed, logsum = lax.map(
        one_row,
        (
            split_heads(query, rows),
            split_heads(keys, rows),
            split_heads(values, rows),
            query_seg,
            key_seg,
        ),
    )
    return (mixed.reshape(query.shape), logsum)


def attend_back(query, keys, values, query_seg, key_seg, logsum, d_mixed, causal):
    rows = query_seg.shape[0]

    def one_row(pack):
        return backward_row(pack[0], pack[1], pack[2], pack[3], pack[4], pack[5], pack[6], causal)

    d_query, d_keys, d_values = lax.map(
        one_row,
        (
            split_heads(query, rows),
            split_heads(keys, rows),
            split_heads(values, rows),
            query_seg,
            key_seg,
            logsum,
            split_heads(d_mixed, rows),
        ),
    )
    return (
        d_query.reshape(query.shape),
        d_keys.reshape(keys.shape),
        d_values.reshape(values.shape),
    )


def local(
    inputs,
    memory,
    tgt_seg,
    src_seg,
    self_query,
    self_key,
    self_value,
    self_out,
    cross_query,
    cross_key,
    cross_value,
    cross_out,
    ffn_in,
    ffn_out,
    norm_gain,
    norm_shift,
    residual_scale,
    cotangent,
):
    stream = inputs.astype(jnp.float32)
    s_mixed, s_logsum = attend_rows(
        project(inputs, self_query),
        project(inputs, self_key),
        project(inputs, self_value),
        tgt_seg,
        tgt_seg,
        True,
    )
    pre1 = residual_scale[0] * stream + branch_total(s_mixed, self_out)
    norm1, first_pull = jax.vjp(layer_norm, pre1, norm_gain[0], norm_shift[0])
    low1 = norm1.astype(jnp.bfloat16)
    c_mixed, c_logsum = attend_rows(
        project(low1, cross_query),
        project(memory, cross_key),
        project(memory, cross_value),
        tgt_seg,
        src_seg,
        False,
    )
    pre2 = residual_scale[1] * norm1 + branch_total(c_mixed, cross_out)
    norm2, second_pull = jax.vjp(layer_norm, pre2, norm_gain[1], norm_shift[1])
    low2 = norm2.astype(jnp.bfloat16)
    upper = jnp.dot(low2, ffn_in, preferred_element_type=jnp.float32)
    act = gelu_tanh(upper).astype(jnp.bfloat16)
    pre3 = residual_scale[2] * norm2 + branch_total(act, ffn_out)
    result, third_pull = jax.vjp(layer_norm, pre3, norm_gain[2], norm_shift[2])
    output = result.astype(jnp.bfloat16)
    d_pre3, gain_three, shift_three = third_pull(cotangent.astype(jnp.float32))
    scale_three = jnp.sum(d_pre3 * norm2, axis=0)
    round_three = d_pre3.astype(jnp.bfloat16)
    upper_again = jnp.dot(low2, ffn_in, preferred_element_type=jnp.float32)
    act_again, gelu_pull = jax.vjp(gelu_tanh, upper_again)
    ffn_out_part = contract_rows(act_again.astype(jnp.bfloat16), round_three)
    d_act = times_rows(round_three, ffn_out)
    d_upper = gelu_pull(d_act)[0].astype(jnp.bfloat16)
    ffn_in_part = contract_rows(low2, d_upper)
    d_norm2 = residual_scale[2] * d_pre3 + stream_total(d_upper, ffn_in)
    d_pre2, gain_two, shift_two = second_pull(d_norm2)
    scale_two = jnp.sum(d_pre2 * norm1, axis=0)
    round_two = d_pre2.astype(jnp.bfloat16)
    cross_out_part = contract_rows(c_mixed, round_two)
    d_cross = times_rows(round_two, cross_out).astype(jnp.bfloat16)
    d_cq, d_ck, d_cv = attend_back(
        project(low1, cross_query),
        project(memory, cross_key),
        project(memory, cross_value),
        tgt_seg,
        src_seg,
        c_logsum,
        d_cross,
        False,
    )
    cross_query_part = contract_rows(low1, d_cq)
    cross_key_part = contract_rows(memory, d_ck)
    cross_value_part = contract_rows(memory, d_cv)
    memory_part = times_rows(d_ck, cross_key) + times_rows(d_cv, cross_value)
    d_norm1 = residual_scale[1] * d_pre2 + stream_total(d_cq, cross_query)
    d_pre1, gain_one, shift_one = first_pull(d_norm1)
    scale_one = jnp.sum(d_pre1 * stream, axis=0)
    round_one = d_pre1.astype(jnp.bfloat16)
    self_out_part = contract_rows(s_mixed, round_one)
    d_self = times_rows(round_one, self_out).astype(jnp.bfloat16)
    d_sq, d_sk, d_sv = attend_back(
        project(inputs, self_query),
        project(inputs, self_key),
        project(inputs, self_value),
        tgt_seg,
        tgt_seg,
        s_logsum,
        d_self,
        True,
    )
    self_query_part = contract_rows(inputs, d_sq)
    self_key_part = contract_rows(inputs, d_sk)
    self_value_part = contract_rows(inputs, d_sv)
    input_part = (
        times_rows(d_sq, self_query) + times_rows(d_sk, self_key) + times_rows(d_sv, self_value)
    )
    width = input_part.shape[1] // lax.axis_size("tensor")
    residual_part = lax.dynamic_slice_in_dim(
        residual_scale[0] * d_pre1, lax.axis_index("tensor") * width, width, 1
    )
    input_grad = (
        lax.psum_scatter(
            input_part.astype(jnp.bfloat16), "tensor", scatter_dimension=1, tiled=True
        ).astype(jnp.float32)
        + residual_part
    )
    memory_grad = lax.psum_scatter(
        memory_part.astype(jnp.bfloat16), "tensor", scatter_dimension=1, tiled=True
    ).astype(jnp.float32)
    (
        sq_sum,
        sk_sum,
        sv_sum,
        so_sum,
        cq_sum,
        ck_sum,
        cv_sum,
        co_sum,
        ffn_in_sum,
        ffn_out_sum,
        gain_grad,
        shift_grad,
        scale_grad,
    ) = (
        lax.psum_scatter(self_query_part, "dp", scatter_dimension=0, tiled=True),
        lax.psum_scatter(self_key_part, "dp", scatter_dimension=0, tiled=True),
        lax.psum_scatter(self_value_part, "dp", scatter_dimension=0, tiled=True),
        lax.psum_scatter(self_out_part, "dp", scatter_dimension=1, tiled=True),
        lax.psum_scatter(cross_query_part, "dp", scatter_dimension=0, tiled=True),
        lax.psum_scatter(cross_key_part, "dp", scatter_dimension=0, tiled=True),
        lax.psum_scatter(cross_value_part, "dp", scatter_dimension=0, tiled=True),
        lax.psum_scatter(cross_out_part, "dp", scatter_dimension=1, tiled=True),
        lax.psum_scatter(ffn_in_part, "dp", scatter_dimension=0, tiled=True),
        lax.psum_scatter(ffn_out_part, "dp", scatter_dimension=1, tiled=True),
        lax.psum_scatter(
            jnp.stack([gain_one, gain_two, gain_three]), "dp", scatter_dimension=1, tiled=True
        ),
        lax.psum_scatter(
            jnp.stack([shift_one, shift_two, shift_three]), "dp", scatter_dimension=1, tiled=True
        ),
        lax.psum_scatter(
            jnp.stack([scale_one, scale_two, scale_three]), "dp", scatter_dimension=1, tiled=True
        ),
    )
    return (
        output,
        input_grad,
        memory_grad,
        sq_sum,
        sk_sum,
        sv_sum,
        so_sum,
        cq_sum,
        ck_sum,
        cv_sum,
        co_sum,
        ffn_in_sum,
        ffn_out_sum,
        gain_grad,
        shift_grad,
        scale_grad,
    )


def solution(mesh):
    return jax.shard_map(
        local,
        mesh=mesh,
        in_specs=(
            P("dp", None),
            P("dp", None),
            P("dp", None),
            P("dp", None),
            P(None, "tensor"),
            P(None, "tensor"),
            P(None, "tensor"),
            P("tensor", None),
            P(None, "tensor"),
            P(None, "tensor"),
            P(None, "tensor"),
            P("tensor", None),
            P(None, "tensor"),
            P("tensor", None),
            P(),
            P(),
            P(),
            P("dp", None),
        ),
        out_specs=(
            P("dp", None),
            P("dp", "tensor"),
            P("dp", "tensor"),
            P("dp", "tensor"),
            P("dp", "tensor"),
            P("dp", "tensor"),
            P("tensor", "dp"),
            P("dp", "tensor"),
            P("dp", "tensor"),
            P("dp", "tensor"),
            P("tensor", "dp"),
            P("dp", "tensor"),
            P("tensor", "dp"),
            P(None, "dp"),
            P(None, "dp"),
            P(None, "dp"),
        ),
        check_vma=False,
    )
```

profile of v0, /device:TPU:0, one launch (start us, length us, event | category | flops | bytes accessed | tf_op | source)
XLA Modules:
  0.0 1468.6 jit_solution(13328778298984462460)
XLA Ops:
  35.5 36.1 %while.52 = (s32[]{:T(128)}, bf16[2,1024,4,64]{1,3,2,0:T(8,128)(2,1)}, f32[2,4,1024]{2,1,0:T(4,128)S(1)}, bf16[2,1024,4,64]{1,3,2,0:T(8,128)(2,1)}, s32[2,1024]{...) while((s32[]{:T(128)}, ...), condition=%wide.region_5.6_spmd, body=%wide.region_0.5_spmd.sunk | while | flops 1128530432 | bytes 71498472 | solution.py:141
  95.6 47.9 %all-reduce.6.cloned.1.call-done = bf16[2048,512]{1,0:T(8,128)(2,1)} async-done(((bf16[2048,512]{1,0:T(8,128)(2,1)}), bf16[2048,512]{1,0:T(8,128)(2,1)}) %all-reduce.6.cloned.1.call-update) | async-done | bytes 2097168 | tf_op jit(solution)/shard_map/psum | solution.py:42
  160.7 35.3 %while.53 = (s32[]{:T(128)}, bf16[2,1024,4,64]{1,3,2,0:T(8,128)(2,1)}, f32[2,4,1024]{2,1,0:T(4,128)S(1)}, bf16[2,1024,4,64]{1,3,2,0:T(8,128)(2,1)}, s32[2,1024]{...) while((s32[]{:T(128)}, ...), condition=%wide.region_14.15_spmd, body=%wide.region_9.14_spmd.sunk | while | flops 1126432768 | bytes 71494384 | solution.py:141
  201.8 63.0 %all-reduce.8.cloned.1.call-done = bf16[2048,512]{1,0:T(8,128)(2,1)} async-done(((bf16[2048,512]{1,0:T(8,128)(2,1)}), bf16[2048,512]{1,0:T(8,128)(2,1)}) %all-reduce.8.cloned.1.call-update) | async-done | bytes 2097168 | tf_op jit(solution)/shard_map/psum | solution.py:42
  283.3 63.0 %all-reduce.10.cloned.1.call-done = bf16[2048,512]{1,0:T(8,128)(2,1)} async-done(((bf16[2048,512]{1,0:T(8,128)(2,1)}), bf16[2048,512]{1,0:T(8,128)(2,1)}) %all-reduce.10.cloned.1.call-update) | async-done | bytes 2097168 | tf_op jit(solution)/shard_map/psum | solution.py:42
  357.2 9.1 fusion.187
  372.3 63.0 %all-reduce.12.cloned.1.call-done = bf16[2048,512]{1,0:T(8,128)(2,1)} async-done(((bf16[2048,512]{1,0:T(8,128)(2,1)}), bf16[2048,512]{1,0:T(8,128)(2,1)}) %all-reduce.12.cloned.1.call-update) | async-done | bytes 2097168 | tf_op jit(solution)/shard_map/psum | solution.py:48
  460.6 73.8 %while.54 = (s32[]{:T(128)}, bf16[2,1024,4,64]{1,3,2,0:T(8,128)(2,1)}, bf16[2,1024,4,64]{1,3,2,0:T(8,128)(2,1)}, bf16[2,1024,4,64]{1,3,2,0:T(8,128)(2,1)}, bf16[...) while((s32[]{:T(128)}, ...), condition=%wide.region_29.30_spmd, body=%wide.region_26.29_spmd.sunk | while | flops 2751197184 | bytes 180010944 | solution.py:160
  546.9 56.4 %all-reduce.14.cloned.1.call-done = bf16[2048,512]{1,0:T(8,128)(2,1)} async-done(((bf16[2048,512]{1,0:T(8,128)(2,1)}), bf16[2048,512]{1,0:T(8,128)(2,1)}) %all-reduce.14.cloned.1.call-update) | async-done | bytes 2097168 | tf_op jit(solution)/shard_map/psum | solution.py:48
  640.7 74.9 %while.55 = (s32[]{:T(128)}, bf16[2,1024,4,64]{1,3,2,0:T(8,128)(2,1)}, bf16[2,1024,4,64]{1,3,2,0:T(8,128)(2,1)}, bf16[2,1024,4,64]{1,3,2,0:T(8,128)(2,1)}, bf16[...) while((s32[]{:T(128)}, ...), condition=%wide.region_36.37_spmd, body=%wide.region_33.36_spmd.sunk | while | flops 2753294848 | bytes 180015024 | solution.py:160
  662.7 8.3 multiply_convert_fusion.8
  780.1 10.1 reduce-scatter.58.cloned.1.call-done
  791.6 31.9 %reduce-scatter.34.cloned.1.call-done = bf16[2048,256]{1,0:T(8,128)(2,1)} async-done(((bf16[2048,512]{1,0:T(8,128)(2,1)}), bf16[2048,256]{1,0:T(8,128)(2,1)}) %reduce-scatter.34.cloned.1.call-update) | async-done | bytes 1048592 | tf_op jit(solution)/shard_map/reduce_scatter | solution.py:288
  826.2 31.8 %reduce-scatter.32.cloned.1.call-done = bf16[2048,256]{1,0:T(8,128)(2,1)} async-done(((bf16[2048,512]{1,0:T(8,128)(2,1)}), bf16[2048,256]{1,0:T(8,128)(2,1)}) %reduce-scatter.32.cloned.1.call-update) | async-done | bytes 1048592 | tf_op jit(solution)/shard_map/reduce_scatter | solution.py:283
  861.4 57.0 %reduce-scatter.40.cloned.1.call-done = f32[256,32]{0,1:T(8,128)} async-done(((f32[256,512]{0,1:T(8,128)}), f32[256,32]{0,1:T(8,128)}) %reduce-scatter.40.cloned.1.call-update) | async-done | bytes 32784 | tf_op jit(solution)/shard_map/reduce_scatter | solution.py:313
  918.4 58.8 %reduce-scatter.54.cloned.1.call-done = f32[32,256]{1,0:T(8,128)} async-done(((f32[512,256]{1,0:T(8,128)}), f32[32,256]{1,0:T(8,128)}) %reduce-scatter.54.cloned.1.call-update) | async-done | bytes 32784
  977.2 59.4 %reduce-scatter.38.cloned.1.call-done = f32[32,256]{1,0:T(8,128)} async-done(((f32[512,256]{1,0:T(8,128)}), f32[32,256]{1,0:T(8,128)}) %reduce-scatter.38.cloned.1.call-update) | async-done | bytes 32784 | tf_op jit(solution)/shard_map/reduce_scatter | solution.py:310
  1036.5 58.8 %reduce-scatter.52.cloned.1.call-done = f32[32,256]{1,0:T(8,128)} async-done(((f32[512,256]{1,0:T(8,128)}), f32[32,256]{1,0:T(8,128)}) %reduce-scatter.52.cloned.1.call-update) | async-done | bytes 32784
  1095.3 65.2 %reduce-scatter.44.cloned.1.call-done = f32[1024,32]{0,1:T(8,128)} async-done(((f32[1024,512]{0,1:T(8,128)}), f32[1024,32]{0,1:T(8,128)}) %reduce-scatter.44.cloned.1.call-update) | async-done | bytes 131088 | tf_op jit(solution)/shard_map/reduce_scatter | solution.py:315
  1160.6 64.8 %reduce-scatter.42.cloned.1.call-done = f32[32,1024]{1,0:T(8,128)} async-done(((f32[512,1024]{1,0:T(8,128)}), f32[32,1024]{1,0:T(8,128)}) %reduce-scatter.42.cloned.1.call-update) | async-done | bytes 131088 | tf_op jit(solution)/shard_map/reduce_scatter | solution.py:314
  1225.3 59.2 %reduce-scatter.36.cloned.1.call-done = f32[256,32]{0,1:T(8,128)} async-done(((f32[256,512]{0,1:T(8,128)}), f32[256,32]{0,1:T(8,128)}) %reduce-scatter.36.cloned.1.call-update) | async-done | bytes 32784 | tf_op jit(solution)/shard_map/reduce_scatter | solution.py:309
  1284.5 58.8 %reduce-scatter.50.cloned.1.call-done = f32[32,256]{1,0:T(8,128)} async-done(((f32[512,256]{1,0:T(8,128)}), f32[32,256]{1,0:T(8,128)}) %reduce-scatter.50.cloned.1.call-update) | async-done | bytes 32784
  1343.4 59.4 %reduce-scatter.46.cloned.1.call-done = f32[32,256]{1,0:T(8,128)} async-done(((f32[512,256]{1,0:T(8,128)}), f32[32,256]{1,0:T(8,128)}) %reduce-scatter.46.cloned.1.call-update) | async-done | bytes 32784
  1402.7 58.8 %reduce-scatter.48.cloned.1.call-done = f32[32,256]{1,0:T(8,128)} async-done(((f32[512,256]{1,0:T(8,128)}), f32[32,256]{1,0:T(8,128)}) %reduce-scatter.48.cloned.1.call-update) | async-done | bytes 32784
  (582 shorter events, 465.2 us)
Async XLA Ops:
  7.2 136.3 %all-reduce.6.cloned.1.call-start = ((), (), s32[]{:S(2)}) async-start(), calls=%async_computation.15 | async-start | bytes 4194304 | tf_op jit(solution)/shard_map/psum | solution.py:42
  77.7 187.1 %all-reduce.8.cloned.1.call-start = ((), (), s32[]{:S(2)}) async-start(), calls=%async_computation.16 | async-start | bytes 4194304 | tf_op jit(solution)/shard_map/psum | solution.py:42
  201.8 144.6 %all-reduce.10.cloned.1.call-start = ((), (), s32[]{:S(2)}) async-start(), calls=%async_computation.17 | async-start | bytes 4194304 | tf_op jit(solution)/shard_map/psum | solution.py:42
  269.0 172.5 %copy-start.79 = (f32[2048]{0:T(1024)}, f32[2048]{0:T(1024)S(1)}, u32[]{:S(2)}) copy-start(f32[2048]{0:T(1024)S(1)} %broadcast_multiply_fusion.1) | copy-start | bytes 24580
  269.8 171.6 %copy-start.85 = (f32[2048]{0:T(1024)}, f32[2048]{0:T(1024)S(1)}, u32[]{:S(2)}) copy-start(f32[2048]{0:T(1024)S(1)} %fusion.205) | copy-start | bytes 24580
  283.3 152.0 %all-reduce.12.cloned.1.call-start = ((), (), s32[]{:S(2)}) async-start(), calls=%async_computation.18 | async-start | bytes 4194304 | tf_op jit(solution)/shard_map/psum | solution.py:48
  357.2 84.3 %copy-start.93 = (f32[2048]{0:T(1024)}, f32[2048]{0:T(1024)S(1)}, u32[]{:S(2)}) copy-start(f32[2048]{0:T(1024)S(1)} %negate_multiply_fusion.2) | copy-start | bytes 24580
  372.2 231.1 %all-reduce.14.cloned.1.call-start = ((), (), s32[]{:S(2)}) async-start(), calls=%async_computation.19 | async-start | bytes 4194304 | tf_op jit(solution)/shard_map/psum | solution.py:48
  540.2 237.2 %reduce-scatter.60.cloned.1.call-start = ((), (), s32[]{:S(2)}) async-start(), calls=%async_computation.34 | async-start | bytes 278528
  541.7 78.6 %copy-start.54 = (bf16[32,8,2,1024]{3,1,2,0:T(8,128)(2,1)}, bf16[32,8,2,1024]{3,1,2,0:T(8,128)(2,1)S(1)}, u32[]{:S(2)}) copy-start(bf16[32,8,2,1024]{3,1,2,0:T(8,128)(2,1)S(1)} %copy.162) | copy-start | bytes 3145732
  618.2 160.5 %reduce-scatter.56.cloned.1.call-start = ((), (), s32[]{:S(2)}) async-start(), calls=%async_computation.32 | async-start | bytes 278528
  619.2 171.1 %reduce-scatter.58.cloned.1.call-start = ((), (), s32[]{:S(2)}) async-start(), calls=%async_computation.33 | async-start | bytes 278528
  620.2 203.3 %reduce-scatter.34.cloned.1.call-start = ((), (), s32[]{:S(2)}) async-start(), calls=%async_computation.21 | async-start | bytes 3145728 | tf_op jit(solution)/shard_map/reduce_scatter | solution.py:288
  624.7 233.3 %reduce-scatter.32.cloned.1.call-start = ((), (), s32[]{:S(2)}) async-start(), calls=%async_computation.20 | async-start | bytes 3145728 | tf_op jit(solution)/shard_map/reduce_scatter | solution.py:283
  725.3 193.1 %reduce-scatter.40.cloned.1.call-start = ((), (), s32[]{:S(2)}) async-start(), calls=%async_computation.24 | async-start | bytes 557056 | tf_op jit(solution)/shard_map/reduce_scatter | solution.py:313
  729.7 247.5 %reduce-scatter.54.cloned.1.call-start = ((), (), s32[]{:S(2)}) async-start(), calls=%async_computation.31 | async-start | bytes 557056
  732.7 303.8 %reduce-scatter.38.cloned.1.call-start = ((), (), s32[]{:S(2)}) async-start(), calls=%async_computation.23 | async-start | bytes 557056 | tf_op jit(solution)/shard_map/reduce_scatter | solution.py:310
  737.9 357.4 %reduce-scatter.52.cloned.1.call-start = ((), (), s32[]{:S(2)}) async-start(), calls=%async_computation.30 | async-start | bytes 557056
  741.6 419.0 %reduce-scatter.44.cloned.1.call-start = ((), (), s32[]{:S(2)}) async-start(), calls=%async_computation.26 | async-start | bytes 2228224 | tf_op jit(solution)/shard_map/reduce_scatter | solution.py:315
  749.2 476.1 %reduce-scatter.42.cloned.1.call-start = ((), (), s32[]{:S(2)}) async-start(), calls=%async_computation.25 | async-start | bytes 2228224 | tf_op jit(solution)/shard_map/reduce_scatter | solution.py:314
  756.8 527.7 %reduce-scatter.36.cloned.1.call-start = ((), (), s32[]{:S(2)}) async-start(), calls=%async_computation.22 | async-start | bytes 557056 | tf_op jit(solution)/shard_map/reduce_scatter | solution.py:309
  760.8 582.6 %reduce-scatter.50.cloned.1.call-start = ((), (), s32[]{:S(2)}) async-start(), calls=%async_computation.29 | async-start | bytes 557056
  766.5 636.2 %reduce-scatter.46.cloned.1.call-start = ((), (), s32[]{:S(2)}) async-start(), calls=%async_computation.27 | async-start | bytes 557056
  772.1 689.5 %reduce-scatter.48.cloned.1.call-start = ((), (), s32[]{:S(2)}) async-start(), calls=%async_computation.28 | async-start | bytes 557056
  (148 other events, 1663.8 us)
Sparse Core Ops, SparseCore 0:
  77.8 65.5 all-reduce.5
  201.9 62.9 all-reduce.7
  283.4 62.9 all-reduce.9
  372.4 62.9 all-reduce.11
  540.3 62.9 all-reduce.13
  618.3 55.3 reduce-scatter.59
  677.6 54.2 reduce-scatter.55
  735.9 54.3 reduce-scatter.57
  792.6 30.8 reduce-scatter.33
  826.2 31.8 reduce-scatter.31
  862.6 55.7 reduce-scatter.39
  922.4 54.7 reduce-scatter.53
  981.7 54.7 reduce-scatter.37
  1040.5 54.7 reduce-scatter.51
  1099.9 60.5 reduce-scatter.43
  1164.7 60.5 reduce-scatter.41
  1229.7 54.7 reduce-scatter.35
  1288.5 54.8 reduce-scatter.49
  1347.9 54.7 reduce-scatter.45
  1406.7 54.8 reduce-scatter.47
where the time goes:
time: 1480 us; the launch traced here: 1470 us
  waiting for transfers between devices  968 us (65%)
  matrix products  243 us (16%)
  local copies, waits for them, and re-layouts  132 us (9%)
  other arithmetic  107 us (7%)
  between operations  15.9 us (1%)
    unnamed x28, waiting for transfers between devices  305 us
    psum x3, waiting for transfers between devices, branch_total(): lax.psum(jnp.dot(mixed, weight, preferred_element_type=jnp.float32).astyp...  174 us
    psum x2, waiting for transfers between devices, stream_total(): lax.psum(times_rows(grad, weight).astype(jnp.bfloat16), 'tensor')  119 us
    reduce_scatter x1, waiting for transfers between devices, local(): lax.psum_scatter(ffn_out_part, 'dp', scatter_dimension=1, tiled=True)  65.2 us
    reduce_scatter x1, waiting for transfers between devices, local(): lax.psum_scatter(ffn_in_part, 'dp', scatter_dimension=0, tiled=True)  64.8 us
    reduce_scatter x1, waiting for transfers between devices, local(): lax.psum_scatter(cross_query_part, 'dp', scatter_dimension=0, tiled=True)  59.4 us
    reduce_scatter x1, waiting for transfers between devices, local(): lax.psum_scatter(self_out_part, 'dp', scatter_dimension=1, tiled=True)  59.2 us
    reduce_scatter x1, waiting for transfers between devices, local(): lax.psum_scatter(cross_out_part, 'dp', scatter_dimension=1, tiled=True)  57 us
  transfers between devices with their start and end apart: 20, of which 18 were waited for; matrix products, arithmetic and copies ran while one was open for 13% of the time, Pallas kernels for 0%

commit v1 on v0

v1 whole, which is shorter than its diff:
```python
import functools

import jax
import jax.numpy as jnp
from jax import lax
from jax.experimental import pallas as pl
from jax.experimental.pallas import tpu as pltpu
from jax.sharding import PartitionSpec as P

HEAD_DIM = 64
QB = 128
KC = 256
GW = 256
EPS = 1e-05
NEG = -1e30
F32 = jnp.float32
BF16 = jnp.bfloat16
VMEM_LIMIT = 60 * 1024 * 1024


def nn(left, right):
    return lax.dot_general(left, right, (((1,), (0,)), ((), ())), preferred_element_type=F32)


def nt(left, right):
    return lax.dot_general(left, right, (((1,), (1,)), ((), ())), preferred_element_type=F32)


def tn(left, right):
    return lax.dot_general(left, right, (((0,), (0,)), ((), ())), preferred_element_type=F32)


def iota(shape, dim):
    return lax.broadcasted_iota(jnp.int32, shape, dim)


def normalise(pre):
    center = jnp.mean(pre, axis=-1, keepdims=True)
    centered = pre - center
    rstd = lax.rsqrt(jnp.mean(centered * centered, axis=-1, keepdims=True) + EPS)
    return centered * rstd, rstd


def norm_back(grad, gain, xhat, rstd):
    scaled = grad * gain
    first = jnp.mean(scaled, axis=-1, keepdims=True)
    second = jnp.mean(scaled * xhat, axis=-1, keepdims=True)
    return rstd * (scaled - first - xhat * second)


def rows_at(block, size):
    return pl.ds(pl.multiple_of(block * size, size), size)


def stack_heads(block):
    head = iota((1, GW), 1) // HEAD_DIM
    return jnp.concatenate(
        [block * (head == h).astype(F32).astype(BF16) for h in range(GW // HEAD_DIM)], axis=0
    )


def unstack_heads(stacked, rows):
    low_half = iota((1, 128), 1) < HEAD_DIM
    tiles = []
    for tile in range(GW // 128):
        cols = slice(tile * 128, tile * 128 + 128)
        first, second = 2 * tile, 2 * tile + 1
        tiles.append(
            jnp.where(
                low_half,
                stacked[first * rows : (first + 1) * rows, cols],
                stacked[second * rows : (second + 1) * rows, cols],
            )
        )
    return jnp.concatenate(tiles, axis=1)


def attend_block(i, q_ref, k_ref, v_ref, lo, hi, first, count, lse_ref, s_scr, m_scr, l_scr, o_scr):
    heads = GW // HEAD_DIM
    groups = q_ref.shape[1] // GW
    rows = rows_at(i, QB)
    stacks = [stack_heads(q_ref[rows, g * GW : (g + 1) * GW]) for g in range(groups)]

    def key_rows(j):
        return pl.multiple_of(first + j * KC, 16)

    def scores(g, j):
        start = key_rows(j)
        place = start + iota((QB, KC), 1)
        allowed = (place >= lo) & (place < hi)
        s = nt(stacks[g], k_ref[pl.ds(start, KC), g * GW : (g + 1) * GW])
        s = jnp.where(allowed[None], s.reshape(heads, QB, KC), NEG).reshape(heads * QB, KC)
        s_scr[g, j] = s
        return jnp.maximum(s[:, :128], s[:, 128:])

    for g in range(groups):
        m_scr[g] = scores(g, 0)

    @pl.loop(1, count)
    def _(j):
        for g in range(groups):
            m_scr[g] = jnp.maximum(m_scr[g], scores(g, j))

    peaks = [jnp.max(m_scr[g], axis=-1, keepdims=True) for g in range(groups)]

    def weigh(g, j):
        p = jnp.exp(s_scr[g, j] - peaks[g])
        o = nn(p.astype(BF16), v_ref[pl.ds(key_rows(j), KC), g * GW : (g + 1) * GW])
        return p[:, :128] + p[:, 128:], o

    for g in range(groups):
        l_scr[g], o_scr[g] = weigh(g, 0)

    @pl.loop(1, count)
    def _(j):
        for g in range(groups):
            more_l, more_o = weigh(g, j)
            l_scr[g] = l_scr[g] + more_l
            o_scr[g] = o_scr[g] + more_o

    lane = iota((1, 128), 1)
    logs = jnp.zeros((QB, 128), F32)
    parts = []
    for g in range(groups):
        total = jnp.sum(l_scr[g], axis=-1, keepdims=True)
        log = peaks[g] + jnp.log(total)
        for h in range(heads):
            logs = jnp.where(lane == g * heads + h, log[h * QB : (h + 1) * QB], logs)
        parts.append(unstack_heads(o_scr[g] * (1.0 / total), QB).astype(BF16))
    lse_ref[:, rows] = jnp.transpose(logs)[: groups * heads]
    return jnp.concatenate(parts, axis=1)


def attend_back_block(
    i, q_ref, k_ref, v_ref, do_ref, lse_ref, delta_ref, lo, hi, first, count, dq_ref, dk_scr, dv_scr, r_scr
):
    heads = GW // HEAD_DIM
    groups = q_ref.shape[1] // GW
    rows = rows_at(i, QB)

    for g in range(groups):
        cols = slice(g * GW, (g + 1) * GW)
        qs = stack_heads(q_ref[rows, cols])
        ds = stack_heads(do_ref[rows, cols])

        def chunk(j):
            start = pl.multiple_of(first + j * KC, 16)
            keys = pl.ds(start, KC)
            kg = k_ref[keys, cols]
            place = start + iota((KC, QB), 0)
            allowed = (place >= lo) & (place < hi)
            st = nt(kg, qs)
            dp = nt(v_ref[keys, cols], ds)
            probs, grads = [], []
            for h in range(heads):
                part = slice(h * QB, (h + 1) * QB)
                row = slice(g * heads + h, g * heads + h + 1)
                p = jnp.where(allowed, jnp.exp(st[:, part] - lse_ref[row, rows]), 0.0)
                probs.append(p.astype(BF16))
                grads.append((p * (dp[:, part] - delta_ref[row, rows])).astype(BF16))
            prob = jnp.concatenate(probs, axis=1)
            grad = jnp.concatenate(grads, axis=1)
            dv_scr[keys, cols] += nn(prob, ds)
            dk_scr[keys, cols] += nn(grad, qs)
            return tn(grad, kg)

        r_scr[g] = chunk(0)

        @pl.loop(1, count)
        def _(j):
            r_scr[g] = r_scr[g] + chunk(j)

        dq_ref[rows, cols] = (unstack_heads(r_scr[g], QB) * HEAD_DIM**-0.5).astype(BF16)


def set_delta(i, do, mixed, delta_scr):
    heads = do.shape[1] // HEAD_DIM
    product = do.astype(F32) * mixed.astype(F32)
    high = product.astype(BF16)
    rest = (product - high.astype(F32)).astype(BF16)
    pick = (iota((heads, do.shape[1]), 1) // HEAD_DIM == iota((heads, do.shape[1]), 0)).astype(F32).astype(BF16)
    delta_scr[:, rows_at(i, QB)] = nt(pick, high) + nt(pick, rest)


def put_transposed(i, block, scr, chunk):
    turned = jnp.transpose(block)
    for n in range(turned.shape[0] // chunk):
        scr[n % 2, (n // 2) * chunk : (n // 2 + 1) * chunk, rows_at(i, QB)] = turned[n * chunk : (n + 1) * chunk]


def add_sum(ref, row, value):
    ref[row : row + 1, :] += jnp.sum(value, axis=0, keepdims=True)


def self_forward(
    sc, x, qo, qx, ko, kx, vo, vx, oo, ox, bcol, gain, shift, omega,
    q, k, v, mixed, lse, xhat, rstd, s_scr, m_scr, l_scr, o_scr,
):
    half = qo.shape[1]
    scale = HEAD_DIM**-0.5

    @pl.loop(0, x.shape[0] // 256)
    def _(i):
        rows = rows_at(i, 256)
        block = x[rows, :]
        for out, own, other, factor in ((q, qo, qx, scale), (k, ko, kx, 1.0), (v, vo, vx, 1.0)):
            out[rows, :half] = (nn(block, own[...]) * factor).astype(BF16)
            out[rows, half:] = (nn(block, other[...]) * factor).astype(BF16)

    blocks = x.shape[0] // QB

    @pl.loop(0, blocks)
    def _(i):
        rows = rows_at(i, QB)
        block = attend_block(
            i, q, k, v, bcol[rows, 0:1], bcol[rows, 1:2], sc[2 + i], sc[2 + blocks + i], lse, s_scr, m_scr, l_scr, o_scr
        )
        mixed[rows, :] = block
        branch = nn(block[:, :half], oo[...]) + nn(block[:, half:], ox[...])
        pre = omega[0:1] * x[rows, :].astype(F32) + branch
        hat, inv = normalise(pre)
        xhat[rows, :] = hat
        rstd[rows, :] = jnp.broadcast_to(inv, (QB, rstd.shape[1]))


def cross_forward(
    sc, xhat1, mem, qo, qx, ko, kx, vo, vx, oo, ox, bcol, gain, shift, omega,
    q, k, v, mixed, lse, xhat, rstd, s_scr, m_scr, l_scr, o_scr,
):
    half = qo.shape[1]
    scale = HEAD_DIM**-0.5

    @pl.loop(0, mem.shape[0] // 256)
    def _(i):
        rows = rows_at(i, 256)
        low1 = (xhat1[rows, :] * gain[0:1] + shift[0:1]).astype(BF16)
        block = mem[rows, :]
        for out, left, own, other, factor in (
            (q, low1, qo, qx, scale), (k, block, ko, kx, 1.0), (v, block, vo, vx, 1.0)
        ):
            out[rows, :half] = (nn(left, own[...]) * factor).astype(BF16)
            out[rows, half:] = (nn(left, other[...]) * factor).astype(BF16)

    blocks = mem.shape[0] // QB

    @pl.loop(0, blocks)
    def _(i):
        rows = rows_at(i, QB)
        block = attend_block(
            i, q, k, v, bcol[rows, 2:3], bcol[rows, 3:4], sc[2 + 2 * blocks + i], sc[2 + 3 * blocks + i],
            lse, s_scr, m_scr, l_scr, o_scr,
        )
        mixed[rows, :] = block
        branch = nn(block[:, :half], oo[...]) + nn(block[:, half:], ox[...])
        pre = omega[1:2] * (xhat1[rows, :] * gain[0:1] + shift[0:1]) + branch
        hat, inv = normalise(pre)
        xhat[rows, :] = hat
        rstd[rows, :] = jnp.broadcast_to(inv, (QB, rstd.shape[1]))


def ffn_forward(
    sc, xhat2, io, ix, oo, ox, cot, gain, shift, omega,
    out, act, slope, d_pre3, sums,
):
    sums[...] = jnp.zeros_like(sums)
    size = 256
    width = 512
    half = io.shape[1]

    @pl.loop(0, xhat2.shape[0] // size)
    def _(i):
        rows = rows_at(i, size)
        norm2 = xhat2[rows, :] * gain[1:2] + shift[1:2]
        low2 = norm2.astype(BF16)
        pre = omega[2:3] * norm2
        for first in range(0, 2 * half, width):
            part = first % half
            win = (io if first < half else ix)[:, part : part + width]
            wout = (oo if first < half else ox)[part : part + width, :]
            u = nn(low2, win)
            square = u * u
            t = jnp.tanh(0.7978845608028654 * u * (1.0 + 0.044715 * square))
            a = (0.5 * u * (1.0 + t)).astype(BF16)
            act[rows, first : first + width] = a
            slope[rows, first : first + width] = (
                0.5 * (1.0 + t)
                + 0.5 * u * (1.0 - t * t) * (0.7978845608028654 * (1.0 + 0.134145 * square))
            ).astype(BF16)
            pre = pre + nn(a, wout)
        hat, inv = normalise(pre)
        out[rows, :] = (hat * gain[2:3] + shift[2:3]).astype(BF16)
        grad = cot[rows, :].astype(F32)
        d_pre = norm_back(grad, gain[2:3], hat, inv)
        d_pre3[rows, :] = d_pre
        add_sum(sums, 0, grad * hat)
        add_sum(sums, 1, grad)
        add_sum(sums, 2, d_pre * norm2)


def ffn_backward(
    sc, d_pre3, act, slope, xhat2, rstd2, io, ix, oo, ox, gain, shift, omega,
    d_pre2, keep_own, keep_oth, send_own, send_oth, sums, up_scr, norm_t, grad_t, *, chunk,
):
    sums[...] = jnp.zeros_like(sums)
    half = io.shape[1]

    @pl.loop(0, xhat2.shape[0] // QB)
    def _(i):
        rows = rows_at(i, QB)
        grad = d_pre3[rows, :]
        low = grad.astype(BF16)
        hat = xhat2[rows, :]
        low2 = (hat * gain[1:2] + shift[1:2]).astype(BF16)
        put_transposed(i, low2, norm_t, chunk)
        put_transposed(i, low, grad_t, chunk)
        total = omega[2:3] * grad
        for side, (win, wout) in enumerate(((io, oo), (ix, ox))):
            up = (slope[rows, side * half : (side + 1) * half].astype(F32) * nt(low, wout[...])).astype(BF16)
            up_scr[rows, side * half : (side + 1) * half] = up
            total = total + nt(up, win[...])
        d_pre2[rows, :] = norm_back(total, gain[1:2], hat, rstd2[rows, 0:1])
        add_sum(sums, 0, total * hat)
        add_sum(sums, 1, total)

    core = sc[1]
    width = 256
    for slot, (own, oth) in enumerate(((keep_own, keep_oth), (send_own, send_oth))):
        place = core if slot == 0 else 1 - core
        for side, out in enumerate((own, oth)):

            @pl.loop(0, half // width)
            def _(n):
                cols = pl.ds(pl.multiple_of(side * half + n * width, width), width)
                out[:, pl.ds(pl.multiple_of(n * width, width), width)] = nn(norm_t[place], up_scr[:, cols]).astype(BF16)
                out[:, pl.ds(pl.multiple_of(half + n * width, width), width)] = nn(grad_t[place], act[:, cols]).astype(
                    BF16
                )


def weight_grads(core, pairs, keep_own, keep_oth, send_own, send_oth):
    for slot, (own, oth) in enumerate(((keep_own, keep_oth), (send_own, send_oth))):
        place = core if slot == 0 else 1 - core
        for n, (left, right) in enumerate(pairs):
            half = right.shape[1] // 2
            own[:, n * half : (n + 1) * half] = nn(left[place], right[:, :half]).astype(BF16)
            oth[:, n * half : (n + 1) * half] = nn(left[place], right[:, half:]).astype(BF16)


def cross_backward(
    sc, d_pre2, q, k, v, mixed, lse, xhat1, rstd1, mem, qo, qx, ko, kx, vo, vx, oo, ox, brow, gain, shift, omega,
    d_pre1, mem_keep, mem_send, keep_own, keep_oth, send_own, send_oth, sums,
    do_scr, delta, dq_scr, dk_scr, dv_scr, dkb, dvb, r_scr, norm_t, mem_t, grad_t, *, chunk,
):
    sums[...] = jnp.zeros_like(sums)
    half = qo.shape[1]
    blocks = mem.shape[0] // QB
    dk_scr[...] = jnp.zeros_like(dk_scr)
    dv_scr[...] = jnp.zeros_like(dv_scr)

    @pl.loop(0, blocks)
    def _(i):
        rows = rows_at(i, QB)
        grad = d_pre2[rows, :]
        low = grad.astype(BF16)
        norm1 = xhat1[rows, :] * gain[0:1] + shift[0:1]
        put_transposed(i, low, grad_t, chunk)
        put_transposed(i, norm1.astype(BF16), norm_t, chunk)
        put_transposed(i, mem[rows, :], mem_t, chunk)
        do = jnp.concatenate([nt(low, oo[...]), nt(low, ox[...])], axis=1).astype(BF16)
        do_scr[rows, :] = do
        set_delta(i, do, mixed[rows, :], delta)
        add_sum(sums, 0, grad * norm1)

    @pl.loop(0, blocks)
    def _(i):
        rows = rows_at(i, QB)
        attend_back_block(
            i, q, k, v, do_scr, lse, delta, brow[2:3, rows], brow[3:4, rows],
            sc[2 + 2 * blocks + i], sc[2 + 3 * blocks + i], dq_scr, dk_scr, dv_scr, r_scr,
        )

    tensor = sc[0]
    mine = pl.ds(pl.multiple_of(tensor * half, half), half)
    theirs = pl.ds(pl.multiple_of((1 - tensor) * half, half), half)

    @pl.loop(0, blocks)
    def _(i):
        rows = rows_at(i, QB)
        dq = dq_scr[rows, :]
        total = omega[1:2] * d_pre2[rows, :] + nt(dq[:, :half], qo[...]) + nt(dq[:, half:], qx[...])
        hat = xhat1[rows, :]
        d_pre1[rows, :] = norm_back(total, gain[0:1], hat, rstd1[rows, 0:1])
        add_sum(sums, 1, total * hat)
        add_sum(sums, 2, total)
        dk = dk_scr[rows, :].astype(BF16)
        dv = dv_scr[rows, :].astype(BF16)
        dkb[rows, :] = dk
        dvb[rows, :] = dv

        def part(which):
            return (
                nt(dk[:, :half], ko[which, :]) + nt(dk[:, half:], kx[which, :])
                + nt(dv[:, :half], vo[which, :]) + nt(dv[:, half:], vx[which, :])
            )

        mem_keep[rows, :] = part(mine)
        mem_send[rows, :] = part(theirs).astype(BF16)

    weight_grads(
        sc[1], ((norm_t, dq_scr), (mem_t, dkb), (mem_t, dvb), (grad_t, mixed)), keep_own, keep_oth, send_own, send_oth
    )


def self_backward(
    sc, d_pre1, q, k, v, mixed, lse, x, qo, qx, ko, kx, vo, vx, oo, ox, brow, omega,
    in_keep, in_send, keep_own, keep_oth, send_own, send_oth, sums,
    do_scr, delta, dq_scr, dk_scr, dv_scr, dkb, dvb, r_scr, in_t, grad_t, *, chunk,
):
    sums[...] = jnp.zeros_like(sums)
    half = qo.shape[1]
    blocks = x.shape[0] // QB
    dk_scr[...] = jnp.zeros_like(dk_scr)
    dv_scr[...] = jnp.zeros_like(dv_scr)

    @pl.loop(0, blocks)
    def _(i):
        rows = rows_at(i, QB)
        grad = d_pre1[rows, :]
        low = grad.astype(BF16)
        block = x[rows, :]
        put_transposed(i, low, grad_t, chunk)
        put_transposed(i, block, in_t, chunk)
        do = jnp.concatenate([nt(low, oo[...]), nt(low, ox[...])], axis=1).astype(BF16)
        do_scr[rows, :] = do
        set_delta(i, do, mixed[rows, :], delta)
        add_sum(sums, 0, grad * block.astype(F32))

    @pl.loop(0, blocks)
    def _(i):
        rows = rows_at(i, QB)
        attend_back_block(
            i, q, k, v, do_scr, lse, delta, brow[0:1, rows], brow[1:2, rows],
            sc[2 + i], sc[2 + blocks + i], dq_scr, dk_scr, dv_scr, r_scr,
        )

    tensor = sc[0]

    @pl.loop(0, blocks)
    def _(i):
        rows = rows_at(i, QB)
        dq = dq_scr[rows, :]
        dk = dk_scr[rows, :].astype(BF16)
        dv = dv_scr[rows, :].astype(BF16)
        dkb[rows, :] = dk
        dvb[rows, :] = dv

        def part(side):
            which = pl.ds(pl.multiple_of(side * half, half), half)
            return (
                nt(dq[:, :half], qo[which, :]) + nt(dq[:, half:], qx[which, :])
                + nt(dk[:, :half], ko[which, :]) + nt(dk[:, half:], kx[which, :])
                + nt(dv[:, :half], vo[which, :]) + nt(dv[:, half:], vx[which, :])
                + omega[0:1, which] * d_pre1[rows, which]
            )

        in_keep[rows, :] = part(tensor)
        in_send[rows, :] = part(1 - tensor).astype(BF16)

    weight_grads(
        sc[1], ((in_t, dq_scr), (in_t, dkb), (in_t, dvb), (grad_t, mixed)), keep_own, keep_oth, send_own, send_oth
    )


def whole_spec(shape):
    return pl.BlockSpec(shape, lambda i, sc: (0,) * len(shape))


def call(body, sc, args, outs, scratch, row_args=(), name=None):
    in_specs = []
    for n, arg in enumerate(args):
        if n in row_args:
            in_specs.append(pl.BlockSpec((row_args[n], arg.shape[1]), lambda i, sc: (sc[0], 0)))
        else:
            in_specs.append(whole_spec(arg.shape))
    return pl.pallas_call(
        body,
        out_shape=[jax.ShapeDtypeStruct(shape, kind) for shape, kind in outs],
        grid_spec=pltpu.PrefetchScalarGridSpec(
            num_scalar_prefetch=1,
            grid=(1,),
            in_specs=in_specs,
            out_specs=[whole_spec(shape) for shape, _ in outs],
            scratch_shapes=[pltpu.VMEM(shape, kind) for shape, kind in scratch],
        ),
        compiler_params=pltpu.CompilerParams(vmem_limit_bytes=VMEM_LIMIT),
        name=name,
    )(sc, *args)


def local(
    inputs, memory, tgt_seg, src_seg, self_query, self_key, self_value, self_out,
    cross_query, cross_key, cross_value, cross_out, ffn_in, ffn_out,
    norm_gain, norm_shift, residual_scale, cotangent, *, n_dp, n_tensor,
):
    d = lax.axis_index("dp")
    t = lax.axis_index("tensor")
    core = d % 2
    length = tgt_seg.shape[1]
    model = inputs.shape[1]
    half = model // n_tensor
    hidden = ffn_in.shape[1]
    blocks = length // QB
    chunk = model // n_dp
    dealt = chunk % 16 == 0
    swap_y = [(0, 1), (1, 0)]

    def swap(n_bit):
        return [(i, i ^ n_bit) for i in range(n_dp)]

    tgt = lax.dynamic_index_in_dim(tgt_seg, t, 0, keepdims=False)
    src = lax.dynamic_index_in_dim(src_seg, t, 0, keepdims=False)
    self_lo = jnp.sum((tgt[None, :] < tgt[:, None]).astype(jnp.int32), axis=1)
    self_hi = jnp.arange(1, length + 1, dtype=jnp.int32)
    cross_lo = jnp.sum((src[None, :] < tgt[:, None]).astype(jnp.int32), axis=1)
    cross_hi = jnp.sum((src[None, :] <= tgt[:, None]).astype(jnp.int32), axis=1)

    def ranges(lo, hi):
        start = lo[::QB] // 16 * 16
        count = (hi[QB - 1 :: QB] - start + KC - 1) // KC
        return jnp.minimum(start, length - count * KC), count

    bounds = jnp.stack([self_lo, self_hi, cross_lo, cross_hi])
    brow = jnp.concatenate([bounds, bounds])
    bcol = bounds.T
    sc = jnp.concatenate(
        [jnp.stack([t, core if dealt else jnp.zeros_like(core)]).astype(jnp.int32), *ranges(self_lo, self_hi),
         *ranges(cross_lo, cross_hi)]
    )

    def fetch(weights, after=None):
        parts = [lax.dynamic_slice_in_dim(w, core * (w.shape[0] // 2), w.shape[0] // 2, 0) for w in weights]
        if after is not None:
            parts, _ = lax.optimization_barrier((parts, after))
        mine = [lax.ppermute(p, "tensor", swap_y) for p in parts]
        other = [lax.ppermute(p, "dp", swap(1)) for p in mine]
        return mine, [
            jnp.where(core == 0, jnp.concatenate([a, b]), jnp.concatenate([b, a])) for a, b in zip(mine, other)
        ]

    s_first, s_oth = fetch((self_query, self_key, self_value, self_out))
    c_first, c_oth = fetch((cross_query, cross_key, cross_value, cross_out), s_first)
    _, (in_oth, out_oth) = fetch((ffn_in, ffn_out), c_first)
    s_weights = []
    for own, oth in zip((self_query, self_key, self_value, self_out), s_oth):
        s_weights += [own, oth]
    c_weights = []
    for own, oth in zip((cross_query, cross_key, cross_value, cross_out), c_oth):
        c_weights += [own, oth]
    f_weights = [ffn_in, in_oth, ffn_out, out_oth]
    norms = [norm_gain, norm_shift, residual_scale]

    wide = (length, model)
    kept = [(wide, BF16)] * 4 + [((model // HEAD_DIM, length), F32), (wide, F32), ((length, 128), F32)]
    heads = GW // HEAD_DIM
    groups = model // GW
    attend_scratch = [
        ((groups, length // KC, heads * QB, KC), F32),
        ((groups, heads * QB, 128), F32),
        ((groups, heads * QB, 128), F32),
        ((groups, heads * QB, GW), F32),
    ]
    q1, k1, v1, mixed1, lse1, xhat1, rstd1 = call(
        self_forward, sc, [inputs, *s_weights, bcol, *norms], kept, attend_scratch, {0: length}, "self_forward"
    )
    q2, k2, v2, mixed2, lse2, xhat2, rstd2 = call(
        cross_forward, sc, [xhat1, memory, *c_weights, bcol, *norms], kept, attend_scratch, {1: length}, "cross_forward"
    )
    sums_shape = ((8, model), F32)
    low_wide = ((length, n_tensor * hidden), BF16)
    out_row, act, slope, d_pre3, sums3 = call(
        ffn_forward, sc, [xhat2, *f_weights, cotangent, *norms],
        [(wide, BF16), low_wide, low_wide, (wide, F32), sums_shape], [], {5: length}, "ffn_forward",
    )
    def grads(width):
        return [((model // 2, width), BF16)] * 4

    turned = ((2, model // 2, length), BF16)
    chunk_rows = chunk if dealt else model // 2
    d_pre2, *f_grads, sums2 = call(
        functools.partial(ffn_backward, chunk=chunk_rows), sc,
        [d_pre3, act, slope, xhat2, rstd2, *f_weights, *norms],
        [(wide, F32), *grads(2 * hidden), sums_shape], [low_wide, turned, turned], {}, "ffn_backward",
    )
    back_scratch = [
        (wide, BF16), ((model // HEAD_DIM, length), F32), (wide, BF16), (wide, F32), (wide, F32), (wide, BF16),
        (wide, BF16), ((groups, heads * QB, GW), F32),
    ]
    halves = [((length, half), F32), ((length, half), BF16)]
    d_pre1, mem_keep, mem_send, *c_grads, sums1 = call(
        functools.partial(cross_backward, chunk=chunk_rows), sc,
        [d_pre2, q2, k2, v2, mixed2, lse2, xhat1, rstd1, memory, *c_weights, brow, *norms],
        [(wide, F32), *halves, *grads(4 * half), sums_shape], [*back_scratch, turned, turned, turned],
        {8: length}, "cross_backward",
    )
    in_keep, in_send, *s_grads, sums0 = call(
        functools.partial(self_backward, chunk=chunk_rows), sc,
        [d_pre1, q1, k1, v1, mixed1, lse1, inputs, *s_weights, brow, residual_scale],
        [*halves, *grads(4 * half), sums_shape], [*back_scratch, turned, turned], {6: length}, "self_backward",
    )

    def both_rows(own, other):
        other = other.astype(own.dtype)
        return jnp.where(t == 0, jnp.concatenate([own, other]), jnp.concatenate([other, own]))

    output = both_rows(out_row, lax.ppermute(out_row, "tensor", swap_y))
    memory_grad = both_rows(mem_keep, lax.ppermute(mem_send, "tensor", swap_y))
    input_grad = both_rows(in_keep, lax.ppermute(in_send, "tensor", swap_y))

    def add(a, b):
        return (a.astype(F32) + b.astype(F32)).astype(BF16)

    def reduce_grads(parts):
        keep_own, keep_oth, send_own, send_oth = parts
        if not dealt:
            own = lax.psum_scatter(
                jnp.concatenate([keep_own, send_own]).astype(F32), "dp", scatter_dimension=0, tiled=True
            )
            oth = lax.psum_scatter(
                jnp.concatenate([keep_oth, send_oth]).astype(F32), "dp", scatter_dimension=0, tiled=True
            )
            return own + lax.ppermute(oth, "tensor", swap_y)
        oth = add(keep_oth, lax.ppermute(send_oth, "dp", swap(1)))
        own = add(keep_own, lax.ppermute(send_own, "dp", swap(1)))
        total = add(own, lax.ppermute(oth, "tensor", swap_y))
        bit = 2
        while bit < n_dp:
            mine = (d // bit) % 2
            dealt_rows = total.reshape(-1, 2, chunk, total.shape[1])
            keep = lax.dynamic_index_in_dim(dealt_rows, mine, 1, keepdims=False)
            send = lax.dynamic_index_in_dim(dealt_rows, 1 - mine, 1, keepdims=False)
            total = keep.astype(F32) + lax.ppermute(send, "dp", swap(bit)).astype(F32)
            bit *= 2
            if bit < n_dp:
                total = total.astype(BF16)
            total = total.reshape(-1, total.shape[-1])
        return total.astype(F32)

    f_sum = reduce_grads(f_grads)
    c_sum = reduce_grads(c_grads)
    s_sum = reduce_grads(s_grads)
    ffn_in_grad, ffn_out_grad = f_sum[:, :hidden], f_sum[:, hidden:].T
    c_out = [c_sum[:, n * half : (n + 1) * half] for n in range(4)]
    s_out = [s_sum[:, n * half : (n + 1) * half] for n in range(4)]

    sums = jnp.concatenate([sums0[0:1], sums1[:3], sums2[:2], sums3[:3]])
    if n_dp & (n_dp - 1):
        sums = lax.psum(sums, ("dp", "tensor"))
    else:
        bit = 1
        while bit < n_dp:
            sums = sums + lax.ppermute(sums, "dp", swap(bit))
            bit *= 2
        sums = sums + lax.ppermute(sums, "tensor", swap_y)
    sums = lax.dynamic_slice_in_dim(sums, d * chunk, chunk, 1)
    gain_grad = jnp.stack([sums[2], sums[4], sums[6]])
    shift_grad = jnp.stack([sums[3], sums[5], sums[7]])
    scale_grad = jnp.stack([sums[0], sums[1], sums[8]])
    return (
        output, input_grad, memory_grad, s_out[0], s_out[1], s_out[2], s_out[3].T, c_out[0], c_out[1], c_out[2],
        c_out[3].T, ffn_in_grad, ffn_out_grad, gain_grad, shift_grad, scale_grad,
    )


def solution(mesh):
    rows, cols = P("dp", None), P(None, "tensor")
    both, turned = P("dp", "tensor"), P("tensor", "dp")
    return jax.shard_map(
        functools.partial(local, n_dp=mesh.shape["dp"], n_tensor=mesh.shape["tensor"]),
        mesh=mesh,
        in_specs=(
            rows, rows, rows, rows, cols, cols, cols, turned_rows(), cols, cols, cols, turned_rows(), cols,
            turned_rows(), P(), P(), P(), rows,
        ),
        out_specs=(
            rows, both, both, both, both, both, turned, both, both, both, turned, both, turned,
            P(None, "dp"), P(None, "dp"), P(None, "dp"),
        ),
        check_vma=False,
    )


def turned_rows():
    return P("tensor", None)
```

time: 1480 us -> 347 us (0.23)
  waiting for transfers between devices: 968 us -> 114 us
  matrix products: 243 us -> 0 us
  Pallas kernels: 0 us -> 144 us
  local copies, waits for them, and re-layouts: 132 us -> 16.9 us
  other arithmetic: 107 us -> 21.8 us
  starting transfers between devices: 1.04 us -> 47.1 us
    reduce_scatter x7 -> x0, waiting for transfers between devices: 369 us -> none  [the longest x1 65.2 us: local(): lax.psum_scatter(ffn_out_part, 'dp', scatter_dimension=1, tiled=True)]
    unnamed x28 -> x0, waiting for transfers between devices: 305 us -> none
    psum x5 -> x0, waiting for transfers between devices: 293 us -> none  [the longest x3 174 us: branch_total(): lax.psum(jnp.dot(mixed, weight, preferred_element_type=jnp.float32).astyp...]
    dot_general x86 -> x0, matrix products: 243 us -> none  [the longest x8 43.3 us: backward_row(): jnp.einsum('qhd,khd->hqk', d_rows, values, preferred_element_type=jnp.flo...]
    pallas_call x0 -> x6, Pallas kernels: none -> 144 us  [call(): pl.pallas_call(body, out_shape=[jax.ShapeDtypeStruct(shape, kind) for sha...]
    ppermute x0 -> x46, waiting for transfers between devices: none -> 114 us  [the longest x3 26.3 us: reduce_grads(): total = add(own, lax.ppermute(oth, 'tensor', swap_y))]
    while x112 -> x0, local copies, waits for them, and re-layouts: 58.9 us -> none  [the longest x8 27.1 us: attend_rows(): lax.map(one_row, (split_heads(query, rows), split_heads(keys, rows), spli...]
    reduce_sum x17 -> x1, other arithmetic: 59.7 us -> 1.38 us  [local(): cross_hi = jnp.sum((src[None, :] <= tgt[:, None]).astype(jnp.int32), axis=1)]
  transfers between devices with their start and end apart: 20 -> 46, of which waited for: 18 -> 20; matrix products, arithmetic and copies ran while one was open for 13% -> 10% of each run, Pallas kernels for 0% -> 10%
where the time goes in v1:
time: 347 us; the launch traced here: 345 us
  Pallas kernels  144 us (41%)
  waiting for transfers between devices  114 us (33%)
  starting transfers between devices  47.1 us (14%)
  other arithmetic  21.8 us (6%)
  local copies, waits for them, and re-layouts  16.9 us (5%)
    pallas_call x6, Pallas kernels, call(): pl.pallas_call(body, out_shape=[jax.ShapeDtypeStruct(shape, kind) for sha...  144 us
    ppermute x3, waiting for transfers between devices, reduce_grads(): total = add(own, lax.ppermute(oth, 'tensor', swap_y))  26.3 us
    ppermute x1, waiting for transfers between devices, local(): output = both_rows(out_row, lax.ppermute(out_row, 'tensor', swap_y))  21.8 us
    ppermute x9, waiting for transfers between devices, reduce_grads(): total = keep.astype(F32) + lax.ppermute(send, 'dp', swap(bit)).astype(F32)  20.6 us
    ppermute x9, starting transfers between devices, reduce_grads(): total = keep.astype(F32) + lax.ppermute(send, 'dp', swap(bit)).astype(F32)  18 us
    ppermute x10, waiting for transfers between devices, fetch(): mine = [lax.ppermute(p, 'tensor', swap_y) for p in parts]  15.1 us
    ppermute x10, starting transfers between devices, fetch(): mine = [lax.ppermute(p, 'tensor', swap_y) for p in parts]  11.5 us
    ppermute x1, waiting for transfers between devices, local(): input_grad = both_rows(in_keep, lax.ppermute(in_send, 'tensor', swap_y))  10.7 us
  transfers between devices with their start and end apart: 46, of which 20 were waited for; matrix products, arithmetic and copies ran while one was open for 10% of the time, Pallas kernels for 10%

profile of v1, /device:TPU:0, one launch (start us, length us, event | category | flops | bytes accessed | tf_op | source)
XLA Modules:
  0.0 345.4 jit_solution(11993929855846010591)
XLA Ops:
  1.8 3.0 collective-permute-start
  24.4 2.7 collective-permute-done.12
  39.3 6.3 %collective-permute-done.16 = bf16[256,1024]{1,0:T(8,128)(2,1)S(1)} collective-permute-done((bf16[256,1024]{1,0:T(8,128)(2,1)S(1)}, bf16[256,1024]{1,0:T(8,128)(2,1)S(1)}, u32[]{:S(2)}, u32[]{:S(2)}) %collective-permute-start.16) | collective-permute-done | bytes 524320 | tf_op jit(solution)/shard_map/ppermute | solution.py:544
  46.5 17.0 %self_forward.1 = (bf16[1024,512]{1,0:T(8,128)(2,1)}, bf16[1024,512]{1,0:T(8,128)(2,1)}, bf16[1024,512]{1,0:T(8,128)(2,1)}, bf16[1024,512]{1,0:T(8,128)(2,1)}, f...) custom-call(s32[34]{0:T(128)} %concatenate.88.sc, bf16[2048,512]{1,0:T(8,128)(2,1)} %x.3, ...), custom_call_target="tpu_custom_call" | custom-call | tf_op jit(solution)/shard_map/self_forward/pallas_call | solution.py:485
  68.8 18.5 %cross_forward.1 = (bf16[1024,512]{1,0:T(8,128)(2,1)}, bf16[1024,512]{1,0:T(8,128)(2,1)}, bf16[1024,512]{1,0:T(8,128)(2,1)}, bf16[1024,512]{1,0:T(8,128)(2,1)}, ...) custom-call(s32[34]{0:T(128)} %concatenate.88.sc, f32[1024,512]{1,0:T(8,128)} %get-tuple-element.62.xhat1, ...), custom_call_target="tpu_custom_call" | custom-call | tf_op jit(solution)/shard_map/cross_forward/pallas_call | solution.py:485
  90.2 19.3 %ffn_forward.1 = (bf16[1024,512]{1,0:T(8,128)(2,1)}, bf16[1024,2048]{1,0:T(8,128)(2,1)}, bf16[1024,2048]{1,0:T(8,128)(2,1)}, f32[1024,512]{1,0:T(8,128)}, f32[8,512]{1,0:T(8,128)}) custom-call(s32[34]{0:T(128)} %concatenate.88.sc, f32[1024,512]{1,0:T(8,128)} %get-tuple-element.67.xhat2, bf16[512,1024]{1,0:T(8,128)(2,1)} %io.3, ...), custom_call_target="tpu_custom_call" | custom-call | tf_op jit(solution)/shard_map/ffn_forward/pallas_call | solution.py:485
  109.6 29.8 %ffn_backward.1 = (f32[1024,512]{1,0:T(8,128)}, bf16[256,2048]{1,0:T(8,128)(2,1)}, bf16[256,2048]{1,0:T(8,128)(2,1)}, bf16[256,2048]{1,0:T(8,128)(2,1)}, bf16[256,2048]{1,0:T(8,128)(2,1)}, /*index=5*/f32[8,512]{1,0:T(8,128)}) custom-call(s32[34]{0:T(128)} %concatenate.88.sc, f32[1024,512]{1,0:T(8,128)} %get-tuple-element.71.d_pre3, ...), custom_call_target="tpu_custom_call" | custom-call | tf_op jit(solution)/shard_map/ffn_backward/pallas_call | solution.py:485
  139.4 30.8 %cross_backward.1 = (f32[1024,512]{1,0:T(8,128)}, f32[1024,256]{1,0:T(8,128)}, bf16[1024,256]{1,0:T(8,128)(2,1)}, bf16[256,1024]{1,0:T(8,128)(2,1)}, bf16[256,10...) custom-call(s32[34]{0:T(128)} %concatenate.88.sc, ...), custom_call_target="tpu_custom_call" | custom-call | tf_op jit(solution)/shard_map/cross_backward/pallas_call | solution.py:485
  170.2 28.8 %self_backward.1 = (f32[1024,256]{1,0:T(8,128)}, bf16[1024,256]{1,0:T(8,128)(2,1)}, bf16[256,1024]{1,0:T(8,128)(2,1)}, bf16[256,1024]{1,0:T(8,128)(2,1)}, bf16[2...) custom-call(s32[34]{0:T(128)} %concatenate.88.sc, f32[1024,512]{1,0:T(8,128)} %get-tuple-element.82.d_pre1, ...), custom_call_target="tpu_custom_call" | custom-call | tf_op jit(solution)/shard_map/self_backward/pallas_call | solution.py:485
  201.9 3.3 collective-permute-start.42
  207.6 3.4 collective-permute-done.43
  211.0 2.6 collective-permute-start.44
  223.5 9.8 %collective-permute-done.22 = bf16[1024,256]{1,0:T(8,128)(2,1)S(1)} collective-permute-done((bf16[1024,256]{1,0:T(8,128)(2,1)}, bf16[1024,256]{1,0:T(8,128)(2,1)S(1)}, u32[]{:S(2)}, u32[]{:S(2)}) %collective-permute-start.22) | collective-permute-done | bytes 524320 | tf_op jit(solution)/shard_map/ppermute | solution.py:616
  233.3 10.7 %collective-permute-done.21 = bf16[1024,256]{1,0:T(8,128)(2,1)S(1)} collective-permute-done((bf16[1024,256]{1,0:T(8,128)(2,1)}, bf16[1024,256]{1,0:T(8,128)(2,1)S(1)}, u32[]{:S(2)}, u32[]{:S(2)}) %collective-permute-start.21) | collective-permute-done | bytes 524320 | tf_op jit(solution)/shard_map/ppermute | solution.py:617
  250.8 21.8 %collective-permute-done.20 = bf16[1024,512]{1,0:T(8,128)(2,1)S(1)} collective-permute-done((bf16[1024,512]{1,0:T(8,128)(2,1)S(1)}, bf16[1024,512]{1,0:T(8,128)(2,1)S(1)}, u32[]{:S(2)}, u32[]{:S(2)}) %collective-permute-start.20) | collective-permute-done | bytes 1048608 | tf_op jit(solution)/shard_map/ppermute | solution.py:615
  276.6 7.2 %collective-permute-done.31 = bf16[256,1024]{1,0:T(8,128)(2,1)S(1)} collective-permute-done((bf16[256,1024]{1,0:T(8,128)(2,1)S(1)}, bf16[256,1024]{1,0:T(8,128)(2,1)S(1)}, u32[]{:S(2)}, u32[]{:S(2)}) %collective-permute-start.31) | collective-permute-done | bytes 524320 | tf_op jit(solution)/shard_map/ppermute | solution.py:634
  286.0 9.0 %collective-permute-done.25 = bf16[256,1024]{1,0:T(8,128)(2,1)S(1)} collective-permute-done((bf16[256,1024]{1,0:T(8,128)(2,1)S(1)}, bf16[256,1024]{1,0:T(8,128)(2,1)S(1)}, u32[]{:S(2)}, u32[]{:S(2)}) %collective-permute-start.25) | collective-permute-done | bytes 524320 | tf_op jit(solution)/shard_map/ppermute | solution.py:634
  297.6 4.3 %collective-permute-done.26 = bf16[4,32,1024]{2,1,0:T(8,128)(2,1)S(1)} collective-permute-done((bf16[4,32,1024]{2,1,0:T(8,128)(2,1)S(1)}, bf16[4,32,1024]{2,1,0:T(8,128)(2,1)S(1)}, u32[]{:S(2)}, u32[]{:S(2)}) %collective-permute-start.26) | collective-permute-done | bytes 262176 | tf_op jit(solution)/shard_map/ppermute | solution.py:641
  306.5 10.1 %collective-permute-done.37 = bf16[256,2048]{1,0:T(8,128)(2,1)S(1)} collective-permute-done((bf16[256,2048]{1,0:T(8,128)(2,1)S(1)}, bf16[256,2048]{1,0:T(8,128)(2,1)S(1)}, u32[]{:S(2)}, u32[]{:S(2)}) %collective-permute-start.37) | collective-permute-done | bytes 1048608 | tf_op jit(solution)/shard_map/ppermute | solution.py:634
  319.1 2.8 collective-permute-start.28
  321.9 8.4 %collective-permute-done.38 = bf16[4,32,2048]{2,1,0:T(8,128)(2,1)S(1)} collective-permute-done((bf16[4,32,2048]{2,1,0:T(8,128)(2,1)S(1)}, bf16[4,32,2048]{2,1,0:T(8,128)(2,1)S(1)}, u32[]{:S(2)}, u32[]{:S(2)}) %collective-permute-start.38) | collective-permute-done | bytes 524320 | tf_op jit(solution)/shard_map/ppermute | solution.py:641
  333.2 4.1 %collective-permute-done.39 = bf16[2,32,2048]{2,1,0:T(8,128)(2,1)S(1)} collective-permute-done((bf16[2,32,2048]{2,1,0:T(8,128)(2,1)S(1)}, bf16[2,32,2048]{2,1,0:T(8,128)(2,1)S(1)}, u32[]{:S(2)}, u32[]{:S(2)}) %collective-permute-start.39) | collective-permute-done | bytes 262176 | tf_op jit(solution)/shard_map/ppermute | solution.py:641
  337.3 2.9 collective-permute-start.40
  340.8 3.8 %collective-permute-done.40 = bf16[1,32,2048]{2,1,0:T(8,128)(2,1)S(1)} collective-permute-done((bf16[1,32,2048]{2,1,0:T(8,128)(2,1)S(1)}, bf16[1,32,2048]{2,1,0:T(8,128)(2,1)S(1)}, u32[]{:S(2)}, u32[]{:S(2)}) %collective-permute-start.40) | collective-permute-done | bytes 131104 | tf_op jit(solution)/shard_map/ppermute | solution.py:641
  (190 shorter events, 84.0 us)
Async XLA Ops:
  1.8 15.9 %collective-permute-start = (bf16[256,256]{1,0:T(8,128)(2,1)S(1)}, bf16[256,256]{1,0:T(8,128)(2,1)S(1)}, u32[]{:S(2)}, u32[]{:S(2)}) collective-permute-start(bf16[256,256]{1,0:T(8,128)(2,1)S(1)} %constant_dynamic-slice_fusion.12), channel_id=1, source_target_pairs={{0,1},{1,0},{2,3},{3,2},{4,5},{5,4},{6,7},{7,6},{8,9},{9,8},{10,11... | collective-permute-start | bytes 393224 | tf_op jit(solution)/shard_map/ppermute | solution.py:544
  22.0 14.1 %collective-permute-start.3 = (bf16[256,256]{1,0:T(8,128)(2,1)S(1)}, bf16[256,256]{1,0:T(8,128)(2,1)S(1)}, u32[]{:S(2)}, u32[]{:S(2)}) collective-permute-start(bf16[256,256]{1,0:T(8,128)(2,1)S(1)} %collective-permute-done.2), channel_id=1, source_target_pairs={{0,2},{2,0},{4,6},{6,4},{8,10},{10,8},{12,14},{14,12},{16,18},{18,... | collective-permute-start | bytes 393224 | tf_op jit(solution)/shard_map/ppermute | solution.py:545
  30.8 14.9 %collective-permute-start.16 = (bf16[256,1024]{1,0:T(8,128)(2,1)S(1)}, bf16[256,1024]{1,0:T(8,128)(2,1)S(1)}, u32[]{:S(2)}, u32[]{:S(2)}) collective-permute-start(bf16[256,1024]{1,0:T(8,128)(2,1)S(1)} %constant_dynamic-slice_fusion.4), channel_id=1, source_target_pairs={{0,1},{1,0},{2,3},{3,2},{4,5},{5,4},{6,7},{7,6},{8,9},{9,8},{10,11... | collective-permute-start | bytes 1572872 | tf_op jit(solution)/shard_map/ppermute | solution.py:544
  32.5 31.6 %collective-permute-start.18 = (bf16[512,512]{1,0:T(8,128)(2,1)S(1)}, bf16[512,512]{1,0:T(8,128)(2,1)S(1)}, u32[]{:S(2)}, u32[]{:S(2)}) collective-permute-start(bf16[512,512]{1,0:T(8,128)(2,1)S(1)} %constant_dynamic-slice_fusion.3), channel_id=1, source_target_pairs={{0,1},{1,0},{2,3},{3,2},{4,5},{5,4},{6,7},{7,6},{8,9},{9,8},{10,11... | collective-permute-start | bytes 1572872 | tf_op jit(solution)/shard_map/ppermute | solution.py:544
  37.3 26.8 %collective-permute-start.11 = (bf16[256,256]{1,0:T(8,128)(2,1)}, bf16[256,256]{1,0:T(8,128)(2,1)S(1)}, u32[]{:S(2)}, u32[]{:S(2)}) collective-permute-start(bf16[256,256]{1,0:T(8,128)(2,1)} %collective-permute-done.10), channel_id=1, source_target_pairs={{0,2},{2,0},{4,6},{6,4},{8,10},{10,8},{12,14},{14,12},{16,18},{18,... | collective-permute-start | bytes 393224 | tf_op jit(solution)/shard_map/ppermute | solution.py:545
  38.2 28.1 %collective-permute-start.13 = (bf16[256,256]{1,0:T(8,128)(2,1)S(1)}, bf16[256,256]{1,0:T(8,128)(2,1)S(1)}, u32[]{:S(2)}, u32[]{:S(2)}) collective-permute-start(bf16[256,256]{1,0:T(8,128)(2,1)S(1)} %collective-permute-done.12), channel_id=1, source_target_pairs={{0,2},{2,0},{4,6},{6,4},{8,10},{10,8},{12,14},{14,12},{16,18},{18,... | collective-permute-start | bytes 393224 | tf_op jit(solution)/shard_map/ppermute | solution.py:545
  45.7 41.6 %collective-permute-start.17 = (bf16[256,1024]{1,0:T(8,128)(2,1)S(1)}, bf16[256,1024]{1,0:T(8,128)(2,1)S(1)}, u32[]{:S(2)}, u32[]{:S(2)}) collective-permute-start(bf16[256,1024]{1,0:T(8,128)(2,1)S(1)} %collective-permute-done.16), channel_id=1, source_target_pairs={{0,2},{2,0},{4,6},{6,4},{8,10},{10,8},{12,14},{14,12},{16,18},{18,... | collective-permute-start | bytes 1572872 | tf_op jit(solution)/shard_map/ppermute | solution.py:545
  64.1 24.7 %collective-permute-start.19 = (bf16[512,512]{1,0:T(8,128)(2,1)S(1)}, bf16[512,512]{1,0:T(8,128)(2,1)S(1)}, u32[]{:S(2)}, u32[]{:S(2)}) collective-permute-start(bf16[512,512]{1,0:T(8,128)(2,1)S(1)} %collective-permute-done.18), channel_id=1, source_target_pairs={{0,2},{2,0},{4,6},{6,4},{8,10},{10,8},{12,14},{14,12},{16,18},{18,... | collective-permute-start | bytes 1572872 | tf_op jit(solution)/shard_map/ppermute | solution.py:545
  217.7 31.2 %collective-permute-start.36 = (bf16[256,2048]{1,0:T(8,128)(2,1)S(1)}, bf16[256,2048]{1,0:T(8,128)(2,1)S(1)}, u32[]{:S(2)}, u32[]{:S(2)}) collective-permute-start(bf16[256,2048]{1,0:T(8,128)(2,1)S(1)} %copy-done.16), channel_id=1, source_target_pairs={{0,2},{2,0},{4,6},{6,4},{8,10},{10,8},{12,14},{14,12},{16,18},{18,... | collective-permute-start | bytes 3145736 | tf_op jit(solution)/shard_map/ppermute | solution.py:632
  217.7 88.8 %collective-permute-start.35 = (bf16[256,2048]{1,0:T(8,128)(2,1)S(1)}, bf16[256,2048]{1,0:T(8,128)(2,1)S(1)}, u32[]{:S(2)}, u32[]{:S(2)}) collective-permute-start(bf16[256,2048]{1,0:T(8,128)(2,1)S(1)} %copy-done.15), channel_id=1, source_target_pairs={{0,2},{2,0},{4,6},{6,4},{8,10},{10,8},{12,14},{14,12},{16,18},{18,... | collective-permute-start | bytes 3145736 | tf_op jit(solution)/shard_map/ppermute | solution.py:633
  218.2 25.9 %collective-permute-start.30 = (bf16[256,1024]{1,0:T(8,128)(2,1)}, bf16[256,1024]{1,0:T(8,128)(2,1)S(1)}, u32[]{:S(2)}, u32[]{:S(2)}) collective-permute-start(bf16[256,1024]{1,0:T(8,128)(2,1)} %get-tuple-element.99), channel_id=1, source_target_pairs={{0,2},{2,0},{4,6},{6,4},{8,10},{10,8},{12,14},{14,12},{16,18},{18,... | collective-permute-start | bytes 1572872 | tf_op jit(solution)/shard_map/ppermute | solution.py:632
  218.3 14.9 %collective-permute-start.22 = (bf16[1024,256]{1,0:T(8,128)(2,1)}, bf16[1024,256]{1,0:T(8,128)(2,1)S(1)}, u32[]{:S(2)}, u32[]{:S(2)}) collective-permute-start(bf16[1024,256]{1,0:T(8,128)(2,1)} %get-tuple-element.91), channel_id=1, source_target_pairs={{0,1},{1,0},{2,3},{3,2},{4,5},{5,4},{6,7},{7,6},{8,9},{9,8},{10,11... | collective-permute-start | bytes 1572872 | tf_op jit(solution)/shard_map/ppermute | solution.py:616
  219.7 24.3 %collective-permute-start.21 = (bf16[1024,256]{1,0:T(8,128)(2,1)}, bf16[1024,256]{1,0:T(8,128)(2,1)S(1)}, u32[]{:S(2)}, u32[]{:S(2)}) collective-permute-start(bf16[1024,256]{1,0:T(8,128)(2,1)} %get-tuple-element.89), channel_id=1, source_target_pairs={{0,1},{1,0},{2,3},{3,2},{4,5},{5,4},{6,7},{7,6},{8,9},{9,8},{10,11... | collective-permute-start | bytes 1572872 | tf_op jit(solution)/shard_map/ppermute | solution.py:617
  233.2 41.6 %collective-permute-start.29 = (bf16[256,1024]{1,0:T(8,128)(2,1)}, bf16[256,1024]{1,0:T(8,128)(2,1)S(1)}, u32[]{:S(2)}, u32[]{:S(2)}) collective-permute-start(bf16[256,1024]{1,0:T(8,128)(2,1)} %get-tuple-element.97), channel_id=1, source_target_pairs={{0,2},{2,0},{4,6},{6,4},{8,10},{10,8},{12,14},{14,12},{16,18},{18,... | collective-permute-start | bytes 1572872 | tf_op jit(solution)/shard_map/ppermute | solution.py:633
  244.1 41.9 %collective-permute-start.23 = (bf16[256,1024]{1,0:T(8,128)(2,1)S(1)}, bf16[256,1024]{1,0:T(8,128)(2,1)S(1)}, u32[]{:S(2)}, u32[]{:S(2)}) collective-permute-start(bf16[256,1024]{1,0:T(8,128)(2,1)S(1)} %copy-done.17), channel_id=1, source_target_pairs={{0,2},{2,0},{4,6},{6,4},{8,10},{10,8},{12,14},{14,12},{16,18},{18,... | collective-permute-start | bytes 1572872 | tf_op jit(solution)/shard_map/ppermute | solution.py:633
  246.5 26.0 %collective-permute-start.20 = (bf16[1024,512]{1,0:T(8,128)(2,1)S(1)}, bf16[1024,512]{1,0:T(8,128)(2,1)S(1)}, u32[]{:S(2)}, u32[]{:S(2)}) collective-permute-start(bf16[1024,512]{1,0:T(8,128)(2,1)S(1)} %copy-done.4), channel_id=1, source_target_pairs={{0,1},{1,0},{2,3},{3,2},{4,5},{5,4},{6,7},{7,6},{8,9},{9,8},{10,11... | collective-permute-start | bytes 3145736 | tf_op jit(solution)/shard_map/ppermute | solution.py:615
  249.0 34.8 %collective-permute-start.31 = (bf16[256,1024]{1,0:T(8,128)(2,1)S(1)}, bf16[256,1024]{1,0:T(8,128)(2,1)S(1)}, u32[]{:S(2)}, u32[]{:S(2)}) collective-permute-start(bf16[256,1024]{1,0:T(8,128)(2,1)S(1)} %add_convert_fusion.4), channel_id=1, source_target_pairs={{0,1},{1,0},{2,3},{3,2},{4,5},{5,4},{6,7},{7,6},{8,9},{9,8},{10,11... | collective-permute-start | bytes 1572872 | tf_op jit(solution)/shard_map/ppermute | solution.py:634
  272.5 22.5 %collective-permute-start.25 = (bf16[256,1024]{1,0:T(8,128)(2,1)S(1)}, bf16[256,1024]{1,0:T(8,128)(2,1)S(1)}, u32[]{:S(2)}, u32[]{:S(2)}) collective-permute-start(bf16[256,1024]{1,0:T(8,128)(2,1)S(1)} %add_convert_fusion.7), channel_id=1, source_target_pairs={{0,1},{1,0},{2,3},{3,2},{4,5},{5,4},{6,7},{7,6},{8,9},{9,8},{10,11... | collective-permute-start | bytes 1572872 | tf_op jit(solution)/shard_map/ppermute | solution.py:634
  274.8 41.7 %collective-permute-start.37 = (bf16[256,2048]{1,0:T(8,128)(2,1)S(1)}, bf16[256,2048]{1,0:T(8,128)(2,1)S(1)}, u32[]{:S(2)}, u32[]{:S(2)}) collective-permute-start(bf16[256,2048]{1,0:T(8,128)(2,1)S(1)} %add_convert_fusion.1), channel_id=1, source_target_pairs={{0,1},{1,0},{2,3},{3,2},{4,5},{5,4},{6,7},{7,6},{8,9},{9,8},{10,11... | collective-permute-start | bytes 3145736 | tf_op jit(solution)/shard_map/ppermute | solution.py:634
  284.1 13.1 %collective-permute-start.32 = (bf16[4,32,1024]{2,1,0:T(8,128)(2,1)S(1)}, bf16[4,32,1024]{2,1,0:T(8,128)(2,1)S(1)}, u32[]{:S(2)}, u32[]{:S(2)}) collective-permute-start(bf16[4,32,1024]{2,1,0:T(8,128)(2,1)S(1)} %dynamic-slice_bitcast_fusion.2), channel_id=1, source_target_pairs={{0,4},{2,6},{4,0},{6,2},{8,12},{10,14},{12,8},{14,10},{16,20},{18,... | collective-permute-start | bytes 786440 | tf_op jit(solution)/shard_map/ppermute | solution.py:641
  302.0 17.0 %collective-permute-start.27 = (bf16[2,32,1024]{2,1,0:T(8,128)(2,1)S(1)}, bf16[2,32,1024]{2,1,0:T(8,128)(2,1)S(1)}, u32[]{:S(2)}, u32[]{:S(2)}) collective-permute-start(bf16[2,32,1024]{2,1,0:T(8,128)(2,1)S(1)} %dynamic-slice_bitcast_fusion.5), channel_id=1, source_target_pairs={{0,8},{2,10},{4,12},{6,14},{8,0},{10,2},{12,4},{14,6},{16,24},{18,... | collective-permute-start | bytes 393224 | tf_op jit(solution)/shard_map/ppermute | solution.py:641
  304.1 17.8 %collective-permute-start.34 = (bf16[1,32,1024]{2,1,0:T(8,128)(2,1)S(1)}, bf16[1,32,1024]{2,1,0:T(8,128)(2,1)S(1)}, u32[]{:S(2)}, u32[]{:S(2)}) collective-permute-start(bf16[1,32,1024]{2,1,0:T(8,128)(2,1)S(1)} %constant_dynamic-slice_fusion.1), channel_id=1, source_target_pairs={{0,16},{2,18},{4,20},{6,22},{8,24},{10,26},{12,28},{14,30},{16,0},... | collective-permute-start | bytes 196616 | tf_op jit(solution)/shard_map/ppermute | solution.py:641
  317.2 13.1 %collective-permute-start.38 = (bf16[4,32,2048]{2,1,0:T(8,128)(2,1)S(1)}, bf16[4,32,2048]{2,1,0:T(8,128)(2,1)S(1)}, u32[]{:S(2)}, u32[]{:S(2)}) collective-permute-start(bf16[4,32,2048]{2,1,0:T(8,128)(2,1)S(1)} %dynamic-slice_bitcast_fusion), channel_id=1, source_target_pairs={{0,4},{2,6},{4,0},{6,2},{8,12},{10,14},{12,8},{14,10},{16,20},{18,... | collective-permute-start | bytes 1572872 | tf_op jit(solution)/shard_map/ppermute | solution.py:641
  319.1 14.0 %collective-permute-start.28 = (bf16[1,32,1024]{2,1,0:T(8,128)(2,1)S(1)}, bf16[1,32,1024]{2,1,0:T(8,128)(2,1)S(1)}, u32[]{:S(2)}, u32[]{:S(2)}) collective-permute-start(bf16[1,32,1024]{2,1,0:T(8,128)(2,1)S(1)} %constant_dynamic-slice_fusion.2), channel_id=1, source_target_pairs={{0,16},{2,18},{4,20},{6,22},{8,24},{10,26},{12,28},{14,30},{16,0},... | collective-permute-start | bytes 196616 | tf_op jit(solution)/shard_map/ppermute | solution.py:641
  (40 other events, 546.0 us)

commit v2 on v0

v2 whole, which is shorter than its diff:
```python
import functools

import jax
import jax.numpy as jnp
from jax import lax
from jax.experimental import pallas as pl
from jax.experimental.pallas import tpu as pltpu
from jax.sharding import PartitionSpec as P

HEAD_DIM = 64
QB = 128
KC = 256
GW = 256
EPS = 1e-05
NEG = -1e30
F32 = jnp.float32
BF16 = jnp.bfloat16
MB = 512
VMEM_LIMIT = 56 * 1024 * 1024
SEGMENTS = 32
FLOPS_PER_US = 9e8


def nn(left, right):
    return lax.dot_general(left, right, (((1,), (0,)), ((), ())), preferred_element_type=F32)


def nt(left, right):
    return lax.dot_general(left, right, (((1,), (1,)), ((), ())), preferred_element_type=F32)


def tn(left, right):
    return lax.dot_general(left, right, (((0,), (0,)), ((), ())), preferred_element_type=F32)


def iota(shape, dim):
    return lax.broadcasted_iota(jnp.int32, shape, dim)


def normalise(pre):
    center = jnp.mean(pre, axis=-1, keepdims=True)
    centered = pre - center
    rstd = lax.rsqrt(jnp.mean(centered * centered, axis=-1, keepdims=True) + EPS)
    return centered * rstd, rstd


def norm_back(grad, gain, xhat, rstd):
    scaled = grad * gain
    first = jnp.mean(scaled, axis=-1, keepdims=True)
    second = jnp.mean(scaled * xhat, axis=-1, keepdims=True)
    return rstd * (scaled - first - xhat * second)


def rows_at(block, size):
    return pl.ds(pl.multiple_of(block * size, size), size)


def stack_heads(block):
    head = iota((1, GW), 1) // HEAD_DIM
    return jnp.concatenate(
        [block * (head == h).astype(F32).astype(BF16) for h in range(GW // HEAD_DIM)], axis=0
    )


def unstack_heads(stacked, rows):
    low_half = iota((1, 128), 1) < HEAD_DIM
    tiles = []
    for tile in range(GW // 128):
        cols = slice(tile * 128, tile * 128 + 128)
        first, second = 2 * tile, 2 * tile + 1
        tiles.append(
            jnp.where(
                low_half,
                stacked[first * rows : (first + 1) * rows, cols],
                stacked[second * rows : (second + 1) * rows, cols],
            )
        )
    return jnp.concatenate(tiles, axis=1)


def attend_units(units, s_scr, m_scr, l_scr, o_scr):
    heads = GW // HEAD_DIM
    stacks = [stack_heads(q[rows_at(i, QB), :]) for i, q, *_ in units]

    def scores(n, j):
        _, _, k, _, lo, hi, first, _ = units[n]
        start = pl.multiple_of(first + j * KC, 128)
        place = start + iota((KC, QB), 0)
        allowed = (place >= lo) & (place < hi)
        s = nt(k[pl.ds(start, KC), :], stacks[n])
        peaks = []
        for h in range(heads):
            part = slice(h * QB, (h + 1) * QB)
            masked = jnp.where(allowed, s[:, part], NEG)
            s_scr[n, j, :, part] = masked
            peaks.append(jnp.max(masked, axis=0, keepdims=True))
        return jnp.concatenate(peaks, axis=1)

    for n in range(len(units)):
        m_scr[n : n + 1, :] = scores(n, 0)
    for n, unit in enumerate(units):

        @pl.loop(1, unit[7])
        def _(j):
            m_scr[n : n + 1, :] = jnp.maximum(m_scr[n : n + 1, :], scores(n, j))

    peaks = [m_scr[n : n + 1, :] for n in range(len(units))]

    def weigh(n, j):
        p = jnp.exp(s_scr[n, j] - peaks[n])
        keys = pl.ds(pl.multiple_of(units[n][6] + j * KC, 128), KC)
        return jnp.sum(p, axis=0, keepdims=True), nn(units[n][3][:, keys], p.astype(BF16))

    for n in range(len(units)):
        l_scr[n : n + 1, :], o_scr[n] = weigh(n, 0)
    for n, unit in enumerate(units):

        @pl.loop(1, unit[7])
        def _(j):
            more_l, more_o = weigh(n, j)
            l_scr[n : n + 1, :] = l_scr[n : n + 1, :] + more_l
            o_scr[n] = o_scr[n] + more_o

    results = []
    for n in range(len(units)):
        total = l_scr[n : n + 1, :]
        log = peaks[n] + jnp.log(total)
        scale = 1.0 / total
        parts = [
            o_scr[n, h * HEAD_DIM : (h + 1) * HEAD_DIM, h * QB : (h + 1) * QB] * scale[:, h * QB : (h + 1) * QB]
            for h in range(heads)
        ]
        mixed = jnp.transpose(jnp.concatenate(parts, axis=0).astype(BF16))
        results.append((mixed, [log[:, h * QB : (h + 1) * QB] for h in range(heads)]))
    return results


def attend_back_units(units, r_scr):
    heads = GW // HEAD_DIM

    def chunk(n, j):
        i, q, k, v, do, lse, delta, lo, hi, first, _, _, dk, dv = units[n]
        rows = rows_at(i, QB)
        keys = pl.ds(pl.multiple_of(first + j * KC, 16), KC)
        qs = stack_heads(q[rows, :])
        ds = stack_heads(do[rows, :])
        kg = k[keys, :]
        place = first + j * KC + iota((KC, QB), 0)
        allowed = (place >= lo) & (place < hi)
        st = nt(kg, qs)
        dp = nt(v[keys, :], ds)
        probs, grads = [], []
        for h in range(heads):
            part = slice(h * QB, (h + 1) * QB)
            p = jnp.where(allowed, jnp.exp(st[:, part] - lse[h : h + 1, rows]), 0.0)
            probs.append(p.astype(BF16))
            grads.append((p * (dp[:, part] - delta[h : h + 1, rows])).astype(BF16))
        prob = jnp.concatenate(probs, axis=1)
        grad = jnp.concatenate(grads, axis=1)
        dv[keys, :] += nn(prob, ds)
        dk[keys, :] += nn(grad, qs)
        return tn(grad, kg)

    for n in range(len(units)):
        r_scr[n] = chunk(n, 0)
    for n, unit in enumerate(units):

        @pl.loop(1, unit[10])
        def _(j):
            r_scr[n] = r_scr[n] + chunk(n, j)

    for n, unit in enumerate(units):
        unit[11][rows_at(unit[0], QB), :] = (unstack_heads(r_scr[n], QB) * HEAD_DIM**-0.5).astype(BF16)


def set_delta(rows, do, mixed, delta_scr):
    heads = do.shape[1] // HEAD_DIM
    product = do.astype(F32) * mixed.astype(F32)
    high = product.astype(BF16)
    rest = (product - high.astype(F32)).astype(BF16)
    pick = (iota((heads, do.shape[1]), 1) // HEAD_DIM == iota((heads, do.shape[1]), 0)).astype(F32).astype(BF16)
    delta_scr[:, rows] = nt(pick, high) + nt(pick, rest)


def put_transposed(rows, block, scr, chunk):
    turned = jnp.transpose(block)
    size = turned.shape[0]
    for n in range(size // chunk):
        first = (n % 2) * (size // 2) + n // 2 * chunk if chunk < size // 2 else n * chunk
        scr[first : first + chunk, rows] = turned[n * chunk : (n + 1) * chunk]


def add_sum(ref, row, value):
    ref[row : row + 1, :] += jnp.sum(value, axis=0, keepdims=True)


def project(rows, left, weight, out, factor=1.0):
    out[rows, :] = (nn(left, weight[...]) * factor).astype(BF16)


def unpack_square(mine, sib, weights):
    core = core_index()
    *cols, out = weights
    part, half = cols[0].shape[0] // 2, out.shape[0]
    small = half // 2
    for place, source in ((core, mine), (1 - core, sib)):
        for n, w in enumerate(cols):
            w[rows_at(place, part), :] = source[n * part : (n + 1) * part, :]
        base = len(cols) * part
        for n in range(out.shape[1] // half):
            out[rows_at(place, small), n * half : (n + 1) * half] = source[
                base + n * small : base + (n + 1) * small, :
            ]


def unpack_ffn(mine, sib, win, wout):
    core = core_index()
    part, rows, width = win.shape[0] // 2, wout.shape[0] // 2, wout.shape[1]
    tiles = win.shape[1] // width
    for place, source in ((core, mine), (1 - core, sib)):
        for n in range(tiles):
            win[rows_at(place, part), n * width : (n + 1) * width] = source[n * part : (n + 1) * part, :]
        wout[rows_at(place, rows), :] = source[tiles * part :, :]


def core_index():
    return lax.axis_index("dp") % 2


def set_ranges(tgt, src, brow, blocks):
    rows, length = tgt.shape
    mine = lax.axis_index("tensor")

    def row(ref):
        value = ref[0:1, :]
        for n in range(1, rows):
            value = jnp.where(mine == n, ref[n : n + 1, :], value)
        return value

    target, source = row(tgt), row(src)
    ids = iota((SEGMENTS, length), 0)

    def before(ids_of, limit):
        count = jnp.sum((ids_of < limit).astype(F32), axis=1, keepdims=True)
        return jnp.sum(jnp.where(ids == target, count, 0.0), axis=0, keepdims=True).astype(jnp.int32)

    values = [
        before(target, ids), iota((1, length), 1) + 1, before(source, ids), before(source, ids + 1)
    ]
    lane = iota((1, 128), 1)
    for n, value in enumerate(values):
        brow[n : n + 1, :] = value
        brow[n + 4 : n + 5, :] = value
    blocks[...] = jnp.zeros_like(blocks)
    for n in range(2):
        first = jnp.zeros((1, 128), jnp.int32)
        last = jnp.zeros((1, 128), jnp.int32)
        for i in range(length // QB):
            low, high = values[2 * n][:, i * QB : i * QB + 1], values[2 * n + 1][:, (i + 1) * QB - 1 : (i + 1) * QB]
            first = jnp.where(lane == i, low, first)
            last = jnp.where(lane == i, high, last)
        first = lax.shift_left(lax.shift_right_logical(first, 7), 7)
        count = lax.shift_right_logical(last - first + (KC - 1), KC.bit_length() - 1)
        blocks[2 * n : 2 * n + 1, :] = jnp.minimum(first, length - count * KC)
        blocks[2 * n + 1 : 2 * n + 2, :] = count


def forward_unit(sc, brow, i, q, k, v, which):
    rows = rows_at(i, QB)
    return (
        i, q, k, v, brow[2 * which : 2 * which + 1, rows], brow[2 * which + 1 : 2 * which + 2, rows],
        sc[2 * which, i], sc[2 * which + 1, i],
    )


def put_logs(lse, i, logs):
    for h, log in enumerate(logs):
        lse[h : h + 1, rows_at(i, QB)] = log


def project_self(x, weights, outs, v_t):
    @pl.loop(0, x.chunks)
    def _(i):
        x.need(i)
        rows = rows_at(i, MB)
        block = x[rows, :]
        for weight, out, factor in zip(weights, outs, (HEAD_DIM**-0.5, 1.0, 1.0)):
            project(rows, block, weight, out, factor)
            out.put(i)
        v_t[:, rows] = jnp.transpose(outs[2][rows, :])


def self_forward_own(sc, qo, ko, vo, x, brow, q, k, v, mixed, lse, v_t, *scratch):
    need(qo, ko, vo)
    project_self(x, (qo, ko, vo), (q, k, v), v_t)
    need(brow)

    @pl.loop(0, x.shape[0] // QB // 2)
    def _(pair):
        pair_of = [2 * pair, 2 * pair + 1]
        units = [forward_unit(sc, brow, i, q, k, v_t, 0) for i in pair_of]
        for i, (block, logs) in zip(pair_of, attend_units(units, *scratch)):
            mixed[rows_at(i, QB), :] = block
            put_logs(lse, i, logs)


def norm_rows(i, pre, xhat, rstd):
    @pl.loop(0, MB // QB)
    def _(n):
        rows = rows_at(i * (MB // QB) + n, QB)
        hat, inv = normalise(pre[rows_at(n, QB), :])
        xhat[rows, :] = hat
        rstd[rows, :] = jnp.broadcast_to(inv, (QB, rstd.shape[1]))

    xhat.put(i)
    rstd.put(i)


def self_forward_rest(
    sc, mine, sib, x, brow, mixed_own, oo, omega,
    q, k, v, mixed, lse, xhat, rstd, qx, kx, vx, ox, pre, v_t, *scratch,
):
    need(mine, sib)
    unpack_square(mine, sib, (qx, kx, vx, ox))
    project_self(x, (qx, kx, vx), (q, k, v), v_t)
    need(brow)

    @pl.loop(0, x.shape[0] // QB // 2)
    def _(pair):
        pair_of = [2 * pair, 2 * pair + 1]
        units = [forward_unit(sc, brow, i, q, k, v_t, 0) for i in pair_of]
        for i, (block, logs) in zip(pair_of, attend_units(units, *scratch)):
            mixed[rows_at(i, QB), :] = block
            put_logs(lse, i, logs)

    need(mixed_own, oo, omega)

    @pl.loop(0, x.chunks)
    def _(i):
        rows = rows_at(i, MB)
        branch = nn(mixed_own[rows, :], oo[...]) + nn(mixed[rows, :], ox[...])
        pre[...] = omega[0:1] * x[rows, :].astype(F32) + branch
        norm_rows(i, pre, xhat, rstd)


def cross_forward(
    sc, mine, sib, qo, ko, vo, gain, shift, xhat1, mem, brow, oo, omega,
    q, k, v, mixed, lse, q_x, k_x, v_x, mixed_x, lse_x, xhat, rstd, qx, kx, vx, ox, pre, v_t, v_xt, *scratch,
):
    need(mine, sib, qo, ko, vo, gain, shift)
    unpack_square(mine, sib, (qx, kx, vx, ox))

    @pl.loop(0, mem.chunks)
    def _(i):
        rows = rows_at(i, MB)
        xhat1.need(i)
        mem.need(i)
        low1 = (xhat1[rows, :] * gain[0:1] + shift[0:1]).astype(BF16)
        block = mem[rows, :]
        for weights, outs, turned in (((qo, ko, vo), (q, k, v), v_t), ((qx, kx, vx), (q_x, k_x, v_x), v_xt)):
            project(rows, low1, weights[0], outs[0], HEAD_DIM**-0.5)
            project(rows, block, weights[1], outs[1])
            project(rows, block, weights[2], outs[2])
            turned[:, rows] = jnp.transpose(outs[2][rows, :])
            for result in outs:
                result.put(i)

    need(brow)

    @pl.loop(0, mem.shape[0] // QB)
    def _(i):
        units = [forward_unit(sc, brow, i, *group, 1) for group in ((q, k, v_t), (q_x, k_x, v_xt))]
        for (block, logs), out, lse_out in zip(attend_units(units, *scratch), (mixed, mixed_x), (lse, lse_x)):
            out[rows_at(i, QB), :] = block
            put_logs(lse_out, i, logs)

    need(oo, omega)

    @pl.loop(0, mem.chunks)
    def _(i):
        rows = rows_at(i, MB)
        branch = nn(mixed[rows, :], oo[...]) + nn(mixed_x[rows, :], ox[...])
        pre[...] = omega[1:2] * (xhat1[rows, :] * gain[0:1] + shift[0:1]) + branch
        norm_rows(i, pre, xhat, rstd)


def ffn_forward(
    sc, io, oo, gain, shift, omega, xhat2, mine, sib, cot,
    out, out_all, act, slope, d_pre3, sums, ix, ox, pre,
):
    need(io, oo, gain, shift, omega, mine, sib)
    unpack_ffn(mine, sib, ix, ox)
    sums[...] = jnp.zeros_like(sums)
    width = 512
    half = io.shape[1]

    @pl.loop(0, xhat2.chunks)
    def _(i):
        rows = rows_at(i, MB)
        xhat2.need(i)
        cot.need(i)
        norm2 = xhat2[rows, :] * gain[1:2] + shift[1:2]
        low2 = norm2.astype(BF16)
        pre[...] = omega[2:3] * norm2
        for side, (win, wout) in enumerate(((io, oo), (ix, ox))):
            for first in range(0, half, width):
                u = nn(low2, win[:, first : first + width])
                square = u * u
                t = jnp.tanh(u * (0.7978845608028654 + (0.7978845608028654 * 0.044715) * square))
                h = 0.5 + 0.5 * t
                a = u * h
                place = slice(side * half + first, side * half + first + width)
                act[rows, place] = a.astype(BF16)
                steep = 2 * 0.7978845608028654 + (6 * 0.7978845608028654 * 0.044715) * square
                slope[rows, place] = (h + a * (1.0 - h) * steep).astype(BF16)
            pre[...] += nn(act[rows, side * half : (side + 1) * half], wout[...])
        act.put(i)
        slope.put(i)

        @pl.loop(0, MB // QB)
        def _(n):
            small = rows_at(i * (MB // QB) + n, QB)
            hat, inv = normalise(pre[rows_at(n, QB), :])
            result = (hat * gain[2:3] + shift[2:3]).astype(BF16)
            out[small, :] = result
            out_all[small, :] = result
            grad = cot[small, :].astype(F32)
            d_pre = norm_back(grad, gain[2:3], hat, inv)
            d_pre3[small, :] = d_pre
            add_sum(sums, 0, grad * hat)
            add_sum(sums, 1, grad)
            add_sum(sums, 2, d_pre * (xhat2[small, :] * gain[1:2] + shift[1:2]))

        for result in (out, out_all, d_pre3):
            result.put(i)


def put_grads(scr, keep, send):
    core = core_index() if keep.dealt else 0
    half = scr.shape[0] // 2
    keep.copy_from(scr.at[rows_at(core, half)])
    send.copy_from(scr.at[rows_at(1 - core, half)])


def ffn_backward(
    sc, oo, io, gain, shift, omega, d_pre3, slope, xhat2, mine, sib, rstd2, act,
    d_pre2, keep, send, sums, up_scr, norm_t, grad_t, ix, ox, acc, grads, *, chunk,
):
    need(io, oo, gain, shift, omega, mine, sib)
    unpack_ffn(mine, sib, ix, ox)
    sums[...] = jnp.zeros_like(sums)
    half = io.shape[1]
    width = 512

    @pl.loop(0, xhat2.chunks)
    def _(i):
        rows = rows_at(i, MB)
        for argument in (d_pre3, slope, xhat2):
            argument.need(i)
        grad = d_pre3[rows, :]
        low = grad.astype(BF16)
        put_transposed(rows, low, grad_t, chunk)
        acc[...] = omega[2:3] * grad
        for side, (win, wout) in enumerate(((io, oo), (ix, ox))):
            for first in range(0, half, width):
                place = slice(side * half + first, side * half + first + width)
                up_scr[rows, place] = (
                    slope[rows, place].astype(F32) * nt(low, wout[first : first + width, :])
                ).astype(BF16)
            acc[...] += nt(up_scr[rows, side * half : (side + 1) * half], win[...])

        if True:
            rstd2.need(i)

        @pl.loop(0, MB // QB)
        def _(n):
            small = rows_at(i * (MB // QB) + n, QB)
            total = acc[rows_at(n, QB), :]
            hat = xhat2[small, :]
            put_transposed(small, (hat * gain[1:2] + shift[1:2]).astype(BF16), norm_t, chunk)
            d_pre2[small, :] = norm_back(total, gain[1:2], hat, rstd2[small, 0:1])
            add_sum(sums, 0, total * hat)
            add_sum(sums, 1, total)

        d_pre2.put(i)

    need(act)
    for side in range(2):
        for left, right, base in ((norm_t, up_scr, 0), (grad_t, act, half)):
            for first in range(0, half, width):
                place = 2 * side * half + base + first
                grads[:, place : place + width] = nn(
                    left[...], right[:, side * half + first : side * half + first + width]
                ).astype(BF16)
    put_grads(grads, keep, send)


def weight_grads(pairs, grads):
    width = grads.shape[1] // 2
    for n, (left, *rights) in enumerate(pairs):
        for side, right in enumerate(rights):
            half = right.shape[1]
            first = side * width + n * half
            grads[:, first : first + half] = nn(left[...], right[...]).astype(BF16)


def backward_unit(sc, brow, i, which, q, k, v, do, lse, delta, dq, dk, dv):
    rows = rows_at(i, QB)
    return (
        i, q, k, v, do, lse, delta, brow[2 * which : 2 * which + 1, rows], brow[2 * which + 1 : 2 * which + 2, rows],
        sc[2 * which, i], sc[2 * which + 1, i], dq, dk, dv,
    )


def attention_grads(low, rows, outs):
    for out, weight, was, total in outs:
        value = nt(low, weight[...]).astype(BF16)
        out[rows, :] = value
        set_delta(rows, value, was[rows, :], total)


def cross_backward(
    sc, mine, sib, oo, gain, shift, omega, d_pre2, xhat1, mem, mixed, mixed_x, q, k, v, q_x, k_x, v_x, lse, lse_x,
    brow, qo, ko, vo, rstd1,
    d_pre1, mem_all, mem_send, keep, send, sums,
    qx, kx, vx, ox, do, do_x, delta, delta_x, dq, dq_x, dk, dk_x, dv, dv_x, dkb, dkb_x, dvb, dvb_x, r_scr,
    grad_t, norm_t, mem_t, acc, grads, *, chunk,
):
    need(mine, sib, oo, gain, shift, omega)
    unpack_square(mine, sib, (qx, kx, vx, ox))
    sums[...] = jnp.zeros_like(sums)
    half = qo.shape[1]
    blocks = mem.shape[0] // QB
    for ref in (dk, dk_x, dv, dv_x):
        ref[...] = jnp.zeros_like(ref)

    @pl.loop(0, mem.chunks)
    def _(i):
        rows = rows_at(i, MB)
        for argument in (d_pre2, xhat1, mem, mixed, mixed_x):
            argument.need(i)
        grad = d_pre2[rows, :]
        low = grad.astype(BF16)
        norm1 = xhat1[rows, :] * gain[0:1] + shift[0:1]
        put_transposed(rows, low, grad_t, chunk)
        put_transposed(rows, norm1.astype(BF16), norm_t, chunk)
        put_transposed(rows, mem[rows, :], mem_t, chunk)
        attention_grads(low, rows, ((do, oo, mixed, delta), (do_x, ox, mixed_x, delta_x)))
        add_sum(sums, 0, grad * norm1)

    need(q, k, v, q_x, k_x, v_x, lse, lse_x, brow)

    @pl.loop(0, blocks)
    def _(i):
        attend_back_units(
            [
                backward_unit(sc, brow, i, 1, q, k, v, do, lse, delta, dq, dk, dv),
                backward_unit(sc, brow, i, 1, q_x, k_x, v_x, do_x, lse_x, delta_x, dq_x, dk_x, dv_x),
            ],
            r_scr,
        )

    need(qo, ko, vo, rstd1)
    tensor = lax.axis_index("tensor")

    @pl.loop(0, mem.chunks)
    def _(i):
        rows = rows_at(i, MB)
        acc[...] = omega[1:2] * d_pre2[rows, :] + nt(dq[rows, :], qo[...]) + nt(dq_x[rows, :], qx[...])
        for low, wide in ((dkb, dk), (dkb_x, dk_x), (dvb, dv), (dvb_x, dv_x)):
            low[rows, :] = wide[rows, :].astype(BF16)

        def part(side):
            which = rows_at(side, half)
            return (
                nt(dkb[rows, :], ko[which, :]) + nt(dkb_x[rows, :], kx[which, :])
                + nt(dvb[rows, :], vo[which, :]) + nt(dvb_x[rows, :], vx[which, :])
            )

        mem_all[rows, :] = part(tensor)
        mem_send[rows, :] = part(1 - tensor).astype(BF16)

        @pl.loop(0, MB // QB)
        def _(n):
            small = rows_at(i * (MB // QB) + n, QB)
            total = acc[rows_at(n, QB), :]
            hat = xhat1[small, :]
            d_pre1[small, :] = norm_back(total, gain[0:1], hat, rstd1[small, 0:1])
            add_sum(sums, 1, total * hat)
            add_sum(sums, 2, total)

        for result in (d_pre1, mem_all, mem_send):
            result.put(i)

    weight_grads(
        ((norm_t, dq, dq_x), (mem_t, dkb, dkb_x), (mem_t, dvb, dvb_x), (grad_t, mixed, mixed_x)), grads
    )
    put_grads(grads, keep, send)


def self_backward(
    sc, mine, sib, oo, d_pre1, x, mixed, mixed_x, q, k, v, q_x, k_x, v_x, lse, lse_x, brow, sums1, sums2, sums3,
    dq, dq_x, dkb, dkb_x, dvb, dvb_x, keep, send,
    qx, kx, vx, ox, do, do_x, delta, delta_x, dk, dk_x, dv, dv_x, r_scr, grad_t, in_t, sums, sums_t, grads, *, chunk,
):
    need(mine, sib, oo)
    unpack_square(mine, sib, (qx, kx, vx, ox))
    blocks = x.shape[0] // QB
    sums[...] = jnp.zeros_like(sums)
    for ref in (dk, dk_x, dv, dv_x):
        ref[...] = jnp.zeros_like(ref)

    @pl.loop(0, x.chunks)
    def _(i):
        rows = rows_at(i, MB)
        for argument in (d_pre1, x, mixed, mixed_x):
            argument.need(i)
        grad = d_pre1[rows, :]
        low = grad.astype(BF16)
        block = x[rows, :]
        put_transposed(rows, low, grad_t, chunk)
        put_transposed(rows, block, in_t, chunk)
        attention_grads(low, rows, ((do, oo, mixed, delta), (do_x, ox, mixed_x, delta_x)))
        add_sum(sums, 0, grad * block.astype(F32))

    need(q, k, v, q_x, k_x, v_x, lse, lse_x, brow, sums1, sums2, sums3)

    @pl.loop(0, blocks)
    def _(i):
        attend_back_units(
            [
                backward_unit(sc, brow, i, 0, q, k, v, do, lse, delta, dq, dk, dv),
                backward_unit(sc, brow, i, 0, q_x, k_x, v_x, do_x, lse_x, delta_x, dq_x, dk_x, dv_x),
            ],
            r_scr,
        )

    for low, wide in ((dkb, dk), (dkb_x, dk_x), (dvb, dv), (dvb_x, dv_x)):
        low[...] = wide[...].astype(BF16)
    sums[1:4, :] = sums1[0:3, :]
    sums[4:6, :] = sums2[0:2, :]
    sums[6:9, :] = sums3[0:3, :]
    put_transposed(pl.ds(0, QB), sums[...].astype(BF16), sums_t, chunk)
    weight_grads(((in_t, dq, dq_x), (in_t, dkb, dkb_x), (in_t, dvb, dvb_x), (grad_t, mixed, mixed_x)), grads)
    width = grads.shape[1] // 2
    for side in range(2):
        grads[:, (side + 1) * width - QB : (side + 1) * width] = sums_t[...]
    put_grads(grads, keep, send)


def input_backward(
    sc, mine, sib, qo, ko, vo, omega, d_pre1, dq, dq_x, dk, dk_x, dv, dv_x, in_all, in_send, qx, kx, vx, ox
):
    need(mine, sib, qo, ko, vo, omega)
    unpack_square(mine, sib, (qx, kx, vx, ox))
    half = qo.shape[1]
    tensor = lax.axis_index("tensor")

    @pl.loop(0, d_pre1.chunks)
    def _(i):
        rows = rows_at(i, MB)
        for argument in (d_pre1, dq, dq_x, dk, dk_x, dv, dv_x):
            argument.need(i)

        def part(side):
            which = rows_at(side, half)
            total = omega[0:1, which] * d_pre1[rows, which]
            for grad, weight in ((dq, qo), (dq_x, qx), (dk, ko), (dk_x, kx), (dv, vo), (dv_x, vx)):
                total = total + nt(grad[rows, :], weight[which, :])
            return total

        in_all[rows, :] = part(tensor)
        in_send[rows, :] = part(1 - tensor).astype(BF16)
        in_all.put(i)
        in_send.put(i)


def fill_kernel(sc, other, out):
    @pl.loop(0, other.chunks)
    def _(i):
        other.need(i)
        rows = rows_at(i, other.shape[0] // other.chunks)
        out[rows, :] = other[rows, :].astype(out.dtype)
        out.put(i)


class Buffer:
    def __init__(self, ref, far, sems, chunks):
        self.ref, self.far, self.sems, self.chunks = ref, far, sems, chunks
        self.shape, self.dtype = far.shape, far.dtype

    def __getitem__(self, index):
        return self.ref[index]

    def __setitem__(self, index, value):
        self.ref[index] = value

    def chunk(self, i):
        size = self.shape[0] // self.chunks
        if self.chunks == 1:
            return self.ref, self.far
        rows = rows_at(i, size)
        return self.ref.at[rows], self.far.at[rows]

    def load(self):
        for i in range(self.chunks):
            near, far = self.chunk(i)
            pltpu.make_async_copy(far, near, self.sems.at[i]).start()

    def need(self, i):
        near, far = self.chunk(i)
        pltpu.make_async_copy(far, near, self.sems.at[i]).wait()

    def put(self, i=0):
        near, far = self.chunk(i)
        pltpu.make_async_copy(near, far, self.sems.at[0]).start()

    def copy_from(self, near):
        pltpu.make_async_copy(near, self.far, self.sems.at[0]).start()

    def done(self):
        pltpu.make_async_copy(self.far, self.far, self.sems.at[0]).wait()


def need(*buffers):
    for buffer in buffers:
        for i in range(buffer.chunks):
            buffer.need(i)


def call(
    body, sc, args, outs, scratch, us, picks=None, puts=None, alias=None, cuts=None, out_cuts=None, bare=(), dealt=True
):
    picks, puts, cuts, out_cuts = picks or {}, puts or {}, cuts or {}, out_cuts or {}

    def block(ref, pick):
        if pick is None:
            return ref
        rows, other = pick
        place = lax.axis_index("tensor")
        return ref.at[rows_at(1 - place if other else place, rows)]

    def size(shape, pick):
        return shape if pick is None else (pick[0], *shape[1:])

    loads = [n for n in range(len(args)) if n != alias]

    def kernel(sc, *refs):
        refs = list(refs)
        ins = [refs.pop(0) for _ in args]
        far_outs = [refs.pop(0) for _ in outs]
        near_ins = [refs.pop(0) for _ in loads]
        near_outs = [None if n in bare else refs.pop(0) for n in range(len(outs))]
        in_sems = [refs.pop(0) for _ in loads]
        out_sems = [refs.pop(0) for _ in outs]
        arguments = [
            Buffer(near, block(ins[n], picks.get(n)), sems, cuts.get(n, 1))
            for n, near, sems in zip(loads, near_ins, in_sems)
        ]
        results = [
            Buffer(near, block(far, puts.get(n)), sems, out_cuts.get(n, 1))
            for n, (far, near, sems) in enumerate(zip(far_outs, near_outs, out_sems))
        ]
        for result in results:
            result.dealt = dealt
        for argument in arguments:
            argument.load()
        body(sc, *arguments, *results, *refs)
        for n, result in enumerate(results):
            if n not in out_cuts and n not in bare:
                result.put()
        for result in results:
            result.done()

    return pl.pallas_call(
        kernel,
        out_shape=[jax.ShapeDtypeStruct(shape, kind) for shape, kind in outs],
        grid_spec=pltpu.PrefetchScalarGridSpec(
            num_scalar_prefetch=1,
            grid=(1,),
            in_specs=[pl.BlockSpec(memory_space=pl.ANY)] * len(args),
            out_specs=[pl.BlockSpec(memory_space=pl.ANY)] * len(outs),
            scratch_shapes=[
                *[pltpu.VMEM(size(args[n].shape, picks.get(n)), args[n].dtype) for n in loads],
                *[pltpu.VMEM(size(shape, puts.get(n)), kind) for n, (shape, kind) in enumerate(outs) if n not in bare],
                *[pltpu.SemaphoreType.DMA((cuts.get(n, 1),)) for n in loads],
                *[pltpu.SemaphoreType.DMA((1,)) for _ in outs],
                *[pltpu.VMEM(shape, kind) for shape, kind in scratch],
            ],
        ),
        input_output_aliases={} if alias is None else {alias + 1: 0},
        cost_estimate=pl.CostEstimate(flops=int(us * FLOPS_PER_US), bytes_accessed=1024, transcendentals=0),
        compiler_params=pltpu.CompilerParams(vmem_limit_bytes=VMEM_LIMIT),
        name=(body.func if isinstance(body, functools.partial) else body).__name__,
    )(sc, *args)


def pack(weights, outs, moves, segments=None):
    extra = [] if segments is None else list(segments)
    length = extra[0].shape[1] if extra else 0
    ranges = [((8, length), jnp.int32), ((8, 128), jnp.int32)] if extra else []

    def pack_weights(*refs):
        refs = list(refs)
        sources = [refs.pop(0) for _ in weights]
        ids = [refs.pop(0) for _ in extra]
        targets = [refs.pop(0) for _ in outs]
        sem = refs.pop()
        core = core_index()
        copies = []
        for n, (which, rows, first, out, start) in enumerate(moves):
            width = outs[out][0][1]
            copies.append(
                pltpu.make_async_copy(
                    sources[which].at[rows_at(core, rows), first : first + width],
                    targets[out].at[start : start + rows, :],
                    sem.at[n],
                )
            )
        for copy in copies:
            copy.start()
        if ids:
            set_ranges(*ids, *refs)
        for copy in copies:
            copy.wait()

    near = pl.BlockSpec(memory_space=pltpu.VMEM)
    return pl.pallas_call(
        pack_weights,
        out_shape=[jax.ShapeDtypeStruct(shape, kind) for shape, kind in outs + ranges],
        in_specs=[pl.BlockSpec(memory_space=pl.ANY)] * len(weights) + [near] * len(extra),
        out_specs=[near] * len(outs + ranges),
        scratch_shapes=[pltpu.SemaphoreType.DMA((len(moves),))],
        cost_estimate=pl.CostEstimate(flops=int(FLOPS_PER_US), bytes_accessed=1024, transcendentals=0),
        compiler_params=pltpu.CompilerParams(vmem_limit_bytes=16 * 1024 * 1024),
        name="pack_weights",
    )(*weights, *extra)


def local(
    inputs, memory, tgt_seg, src_seg, self_query, self_key, self_value, self_out,
    cross_query, cross_key, cross_value, cross_out, ffn_in, ffn_out,
    norm_gain, norm_shift, residual_scale, cotangent, *, n_dp, n_tensor,
):
    d = lax.axis_index("dp")
    t = lax.axis_index("tensor")
    length = tgt_seg.shape[1]
    model = inputs.shape[1]
    half = model // n_tensor
    hidden = ffn_in.shape[1]
    blocks = length // QB
    chunk = model // n_dp
    dealt = chunk % 16 == 0 and n_dp & (n_dp - 1) == 0
    swap_y = [(0, 1), (1, 0)]

    def swap(n_bit):
        return [(i, i ^ n_bit) for i in range(n_dp)]

    def after(value, *others):
        return lax.optimization_barrier((value, others))[0]

    own_s = [self_query, self_key, self_value, self_out]
    own_c = [cross_query, cross_key, cross_value, cross_out]
    own_f = [ffn_in, ffn_out]
    square = ((4 * half, half), BF16)

    def square_moves(base, out):
        part = model // 2
        moves = [(base + n, part, 0, out, n * part) for n in range(3)]
        return moves + [(base + 3, half // 2, n * half, out, 3 * part + n * half // 2) for n in range(n_tensor)]

    (pack_s,) = pack(own_s, [square], square_moves(0, 0))
    tiles = hidden // model
    pack_c, pack_f, brow, sc = pack(
        own_c + own_f, [square, ((tiles * half + hidden // 2, model), BF16)],
        square_moves(0, 0)
        + [(4, model // 2, n * model, 1, n * model // 2) for n in range(tiles)]
        + [(5, hidden // 2, 0, 1, tiles * model // 2)],
        (tgt_seg, src_seg),
    )
    mine_s = lax.ppermute(pack_s, "tensor", swap_y)

    def fill(whole, other):
        (result,) = call(
            fill_kernel, sc, [whole, other], [(whole.shape, whole.dtype)], [], 1, None, {0: (length, True)}, 0,
            cuts={1: 4}, out_cuts={0: 4},
        )
        return result

    def total(*parts):
        if not dealt:
            return jnp.concatenate(parts)
        result = parts[0].astype(F32)
        for part in parts[1:]:
            result = result + part.astype(F32)
        return result

    def core_send(send):
        return lax.ppermute(send, "dp", swap(1)) if dealt else send

    def near_send(keep):
        if not dealt:
            return keep
        width = keep.shape[1] // 2
        mine = (d // 2) % 2
        near = keep.reshape(-1, 2, chunk, 2 * width)
        here = lax.dynamic_index_in_dim(near, mine, 1, keepdims=False)
        there = lax.dynamic_index_in_dim(near, 1 - mine, 1, keepdims=False)
        across = [(i * 2 + j, (i ^ 2) * 2 + 1 - j) for i in range(n_dp) for j in range(2)]
        return (
            here[..., :width],
            lax.ppermute(there[..., width:], ("dp", "tensor"), across),
            lax.ppermute(here[..., width:], "tensor", swap_y),
            lax.ppermute(there[..., :width], "dp", swap(2)),
        )

    def near_sum(near):
        return total(*near).astype(BF16) if dealt else near

    def far_send(part):
        if not dealt:
            return part
        far = n_dp // 4
        row = d // 4
        parts = [lax.dynamic_index_in_dim(part, row, 0, keepdims=False)]
        for step in range(1, far):
            perm = [(i, i % 4 + (i // 4 + step) % far * 4) for i in range(n_dp)]
            out = lax.dynamic_index_in_dim(part, (row + step) % far, 0, keepdims=False)
            parts.append(lax.ppermute(out, "dp", perm))
        return parts

    def far_sum(parts):
        if dealt:
            return total(*parts)
        return reduce_any(parts)

    def reduce_any(grad):
        grad = lax.psum_scatter(grad.astype(F32), "dp", scatter_dimension=0, tiled=True)
        width = grad.shape[1] // 2
        return grad[:, :width] + lax.ppermute(grad[:, width:], "tensor", swap_y)

    wide, side = (length, model), (length, half)
    heads = GW // HEAD_DIM
    group = [(side, BF16)] * 4 + [((half // HEAD_DIM, length), F32)]
    square_weights = [((model, half), BF16)] * 3 + [((half, model), BF16)]
    stats = [(wide, F32), ((length, 128), F32)]
    attend_scratch = [
        ((2, length // KC, KC, heads * QB), F32),
        ((2, heads * QB), F32),
        ((2, heads * QB), F32),
        ((2, GW, heads * QB), F32),
    ]
    turned_side, block_wide = ((half, length), BF16), ((MB, model), F32)
    cut = length // MB
    norms = [norm_gain, norm_shift, residual_scale]
    s_own = call(
        self_forward_own, sc, [*own_s[:3], inputs, brow], group, [turned_side, *attend_scratch], 7, {3: (length, False)},
        cuts={3: cut}, out_cuts={0: cut, 1: cut, 2: cut},
    )
    s_own, mine_s = lax.optimization_barrier((s_own, mine_s))
    sib_s = lax.ppermute(mine_s, "dp", swap(1))
    mine_c = lax.ppermute(after(pack_c, mine_s), "tensor", swap_y)
    s_rest_stats = call(
        self_forward_rest, sc, [mine_s, sib_s, inputs, brow, s_own[3], self_out, residual_scale], group + stats,
        [*square_weights, block_wide, turned_side, *attend_scratch], 8, {2: (length, False)},
        cuts={2: cut}, out_cuts={n: cut for n in (0, 1, 2, 5, 6)},
    )
    s_rest_stats, mine_c = lax.optimization_barrier((s_rest_stats, mine_c))
    *s_rest, xhat1, rstd1 = s_rest_stats
    sib_c = lax.ppermute(mine_c, "dp", swap(1))
    mine_f = lax.ppermute(after(pack_f, mine_c), "tensor", swap_y)
    c_stats = call(
        cross_forward, sc,
        [mine_c, sib_c, *own_c[:3], norm_gain, norm_shift, xhat1, memory, brow, cross_out, residual_scale],
        group + group + stats,
        [*square_weights, block_wide, turned_side, turned_side, *attend_scratch], 14, {8: (length, False)}, cuts={7: cut, 8: cut},
        out_cuts={n: cut for n in (0, 1, 2, 5, 6, 7, 10, 11)},
    )
    c_stats, mine_f = lax.optimization_barrier((c_stats, mine_f))
    *c_state, xhat2, rstd2 = c_stats
    sib_f = lax.ppermute(mine_f, "dp", swap(1))
    sums_shape = ((8, model), F32)
    low_wide = ((length, n_tensor * hidden), BF16)
    f_weights = [((model, hidden), BF16), ((hidden, model), BF16)]
    out_row, output, act, slope, d_pre3, sums3 = call(
        ffn_forward, sc, [*own_f, *norms, xhat2, mine_f, sib_f, cotangent],
        [(wide, BF16), ((n_tensor * length, model), BF16), low_wide, low_wide, (wide, F32), sums_shape],
        [*f_weights, block_wide], 12,
        {8: (length, False)}, {1: (length, False)}, cuts={5: cut, 8: cut}, out_cuts={n: cut for n in range(5)},
    )
    out_other = lax.ppermute(out_row, "tensor", swap_y)

    def grads(width):
        return [((model // 2, 2 * width), BF16)] * 2

    turned = ((model, length), BF16)
    chunk_rows = chunk if dealt else model // 2
    back, out_other = lax.optimization_barrier((
        call(
            functools.partial(ffn_backward, chunk=chunk_rows), sc,
            [ffn_out, ffn_in, *norms, d_pre3, slope, xhat2, mine_f, sib_f, rstd2, act],
            [(wide, F32), *grads(2 * hidden), sums_shape],
            [low_wide, turned, turned, *f_weights, block_wide, ((model, 4 * hidden), BF16)], 18,
            cuts={n: cut for n in (5, 6, 7, 10)}, out_cuts={0: cut}, bare=(1, 2), dealt=dealt,
        ),
        out_other,
    ))
    d_pre2, f_keep, f_send, sums2 = back
    f_other = core_send(f_send)
    output = fill(output, out_other)
    f_total = total(f_keep, f_other).astype(BF16)
    f_near = near_send(f_total)
    logs = ((half // HEAD_DIM, length), F32)
    halves = [((n_tensor * length, half), F32), (side, BF16)]
    back, f_near = lax.optimization_barrier((
        call(
            functools.partial(cross_backward, chunk=chunk_rows), sc,
            [mine_c, sib_c, cross_out, *norms, after(d_pre2, f_total, output), xhat1, memory, c_state[3], c_state[8],
             *c_state[:3], *c_state[5:8], c_state[4], c_state[9], brow, *own_c[:3], rstd1],
            [(wide, F32), *halves, *grads(4 * half), sums_shape],
            [*square_weights, *[(side, BF16)] * 2, logs, logs, *[(side, BF16)] * 2, *[(side, F32)] * 4,
             *[(side, BF16)] * 4, ((2, heads * QB, GW), F32), turned, turned, turned, block_wide,
             ((model, 8 * half), BF16)],
            22, {8: (length, False)}, {1: (length, False)}, cuts={n: cut for n in range(6, 11)},
            out_cuts={n: cut for n in range(3)}, bare=(3, 4), dealt=dealt,
        ),
        f_near,
    ))
    d_pre1, memory_grad, mem_send, c_keep, c_send, sums1 = back
    mem_other = lax.ppermute(mem_send, "tensor", swap_y)
    c_other = core_send(c_send)
    f_part = near_sum(f_near)
    c_total = total(c_keep, c_other).astype(BF16)
    c_near, f_far = near_send(c_total), far_send(f_part)
    back, c_near, f_far, mem_other = lax.optimization_barrier((
        call(
            functools.partial(self_backward, chunk=chunk_rows), sc,
            [mine_s, sib_s, self_out, after(d_pre1, c_total, f_part), inputs, s_own[3], s_rest[3], *s_own[:3],
             *s_rest[:3], s_own[4], s_rest[4], brow, sums1, sums2, sums3],
            [*[(side, BF16)] * 6, *grads(4 * half + QB)],
            [*square_weights, *[(side, BF16)] * 2, logs, logs, *[(side, F32)] * 4,
             ((2, heads * QB, GW), F32), turned, turned, ((QB, model), F32), ((model, QB), BF16),
             ((model, 2 * (4 * half + QB)), BF16)],
            16, {4: (length, False)}, cuts={n: cut for n in range(3, 7)}, bare=(6, 7), dealt=dealt,
        ),
        c_near, f_far, mem_other,
    ))
    *d_self, s_keep, s_send = back
    s_other = core_send(s_send)
    c_part = near_sum(c_near)
    c_far = far_send(c_part)
    back, c_far, s_other = lax.optimization_barrier((
        call(
            input_backward, sc, [mine_s, sib_s, *own_s[:3], residual_scale, after(d_pre1, c_part), *d_self], halves,
            square_weights, 5, None, {0: (length, False)}, cuts={n: cut for n in range(6, 13)},
            out_cuts={0: cut, 1: cut},
        ),
        c_far, s_other,
    ))
    input_grad, in_send = back
    s_near = near_send(total(s_keep, s_other).astype(BF16))
    in_other = lax.ppermute(in_send, "tensor", swap_y)
    memory_grad = fill(memory_grad, mem_other)
    f_sum, c_sum = far_sum(f_far), far_sum(c_far)
    s_sum = far_sum(far_send(near_sum(s_near)))
    input_grad = fill(input_grad, in_other)
    ffn_in_grad, ffn_out_grad = f_sum[:, :hidden], f_sum[:, hidden:].T
    c_out = [c_sum[:, n * half : (n + 1) * half] for n in range(4)]
    s_out = [s_sum[:, n * half : (n + 1) * half] for n in range(4)]
    sums = s_sum[:, 4 * half : 4 * half + 9].T
    gain_grad = jnp.stack([sums[2], sums[4], sums[6]])
    shift_grad = jnp.stack([sums[3], sums[5], sums[7]])
    scale_grad = jnp.stack([sums[0], sums[1], sums[8]])
    return (
        output, input_grad, memory_grad, s_out[0], s_out[1], s_out[2], s_out[3].T, c_out[0], c_out[1], c_out[2],
        c_out[3].T, ffn_in_grad, ffn_out_grad, gain_grad, shift_grad, scale_grad,
    )


def solution(mesh):
    rows, cols = P("dp", None), P(None, "tensor")
    both, turned = P("dp", "tensor"), P("tensor", "dp")
    return jax.shard_map(
        functools.partial(local, n_dp=mesh.shape["dp"], n_tensor=mesh.shape["tensor"]),
        mesh=mesh,
        in_specs=(
            rows, rows, rows, rows, cols, cols, cols, turned_rows(), cols, cols, cols, turned_rows(), cols,
            turned_rows(), P(), P(), P(), rows,
        ),
        out_specs=(
            rows, both, both, both, both, both, turned, both, both, both, turned, both, turned,
            P(None, "dp"), P(None, "dp"), P(None, "dp"),
        ),
        check_vma=False,
    )


def turned_rows():
    return P("tensor", None)
```

time: 1480 us -> 227 us (0.15)
  waiting for transfers between devices: 968 us -> 38.3 us
  matrix products: 243 us -> 0 us
  Pallas kernels: 0 us -> 130 us
  local copies, waits for them, and re-layouts: 132 us -> 14.2 us
  other arithmetic: 107 us -> 4.75 us
  starting transfers between devices: 1.04 us -> 38.4 us
    reduce_scatter x7 -> x0, waiting for transfers between devices: 369 us -> none  [the longest x1 65.2 us: local(): lax.psum_scatter(ffn_out_part, 'dp', scatter_dimension=1, tiled=True)]
    unnamed x28 -> x0, waiting for transfers between devices: 305 us -> none
    psum x5 -> x0, waiting for transfers between devices: 293 us -> none  [the longest x3 174 us: branch_total(): lax.psum(jnp.dot(mixed, weight, preferred_element_type=jnp.float32).astyp...]
    dot_general x86 -> x0, matrix products: 243 us -> none  [the longest x8 43.3 us: backward_row(): jnp.einsum('qhd,khd->hqk', d_rows, values, preferred_element_type=jnp.flo...]
    pallas_call x0 -> x13, Pallas kernels: none -> 130 us  [the longest x11 128 us: call(): pl.pallas_call(kernel, out_shape=[jax.ShapeDtypeStruct(shape, kind) for s...]
    reduce_sum x17 -> x0, other arithmetic: 59.7 us -> none  [the longest x4 18.5 us: forward_row(): total = jnp.sum(weights, axis=-1, keepdims=True)]
    while x112 -> x0, local copies, waits for them, and re-layouts: 58.9 us -> none  [the longest x8 27.1 us: attend_rows(): lax.map(one_row, (split_heads(query, rows), split_heads(keys, rows), spli...]
    ppermute x0 -> x30, starting transfers between devices: none -> 38.4 us  [the longest x9 12.5 us: far_send(): parts.append(lax.ppermute(out, 'dp', perm))]
  transfers between devices with their start and end apart: 20 -> 30, of which waited for: 18 -> 16; matrix products, arithmetic and copies ran while one was open for 13% -> 3% of each run, Pallas kernels for 0% -> 49%
where the time goes in v2:
time: 227 us
  Pallas kernels  130 us (57%)
  starting transfers between devices  38.4 us (17%)
  waiting for transfers between devices  38.3 us (17%)
  local copies, waits for them, and re-layouts  14.2 us (6%)
  other arithmetic  4.75 us (2%)
    pallas_call x11, Pallas kernels, call(): pl.pallas_call(kernel, out_shape=[jax.ShapeDtypeStruct(shape, kind) for s...  128 us
    ppermute x9, starting transfers between devices, far_send(): parts.append(lax.ppermute(out, 'dp', perm))  12.5 us
    unnamed x58, local copies, waits for them, and re-layouts  10.8 us
    ppermute x3, starting transfers between devices, near_send(): lax.ppermute(there[..., :width], 'dp', swap(2))  7.14 us
    ppermute x9, waiting for transfers between devices, far_send(): parts.append(lax.ppermute(out, 'dp', perm))  6.96 us
    ppermute x1, waiting for transfers between devices, local(): in_other = lax.ppermute(in_send, 'tensor', swap_y)  6.45 us
    ppermute x1, waiting for transfers between devices, local(): mine_f = lax.ppermute(after(pack_f, mine_c), 'tensor', swap_y)  4.76 us
    ppermute x3, waiting for transfers between devices, near_send(): lax.ppermute(there[..., :width], 'dp', swap(2))  4.6 us
  transfers between devices with their start and end apart: 30, of which 16 were waited for; matrix products, arithmetic and copies ran while one was open for 3% of the time, Pallas kernels for 49%

profile of v2, /device:TPU:0, one launch (start us, length us, event | category | flops | bytes accessed | tf_op | source)
XLA Modules:
  0.0 226.9 jit_solution(13697437392950293713)
XLA Ops:
  5.2 3.0 %collective-permute-start = (bf16[1024,256]{1,0:T(8,128)(2,1)S(1)}, bf16[1024,256]{1,0:T(8,128)(2,1)S(1)}, u32[]{:S(2)}, u32[]{:S(2)}) collective-permute-start(bf16[1024,256]{1,0:T(8,128)(2,1)S(1)} %pack_weights.3), channel_id=1, source_target_pairs={{0,1},{1,0},{2,3},{3,2},{4,5},{5,4},{6,7},{7,6},{8,9},{9,8},{10,11... | collective-permute-start | bytes 1572872 | tf_op jit(solution)/shard_map/ppermute | solution.py:881
  10.5 7.5 %self_forward_own.1 = (bf16[1024,256]{1,0:T(8,128)(2,1)}, bf16[1024,256]{1,0:T(8,128)(2,1)}, bf16[1024,256]{1,0:T(8,128)(2,1)}, bf16[1024,256]{1,0:T(8,128)(2,1)}, f32[4,1024]{1,0:T(4,128)}) custom-call(s32[8,128]{1,0:T(8,128)} %copy-done, bf16[512,256]{1,0:T(8,128)(2,1)} %refs_2_.19, bf16[512,256]{1,0:T(8,128)(2,1)} %refs_3_.15, bf16[512,256]{1,0:T(8,128)(2,1)} %refs_4_.13, ...), custom_call_target="tpu_custom_call" | custom-call | flops 6300000256 | bytes 1024 | tf_op jit(solution)/shard_map/self_forward_own/pallas_call | solution.py:775
  22.9 10.5 %self_forward_rest.1 = (bf16[1024,256]{1,0:T(8,128)(2,1)}, bf16[1024,256]{1,0:T(8,128)(2,1)}, bf16[1024,256]{1,0:T(8,128)(2,1)}, bf16[1024,256]{1,0:T(8,128)(2,1...) custom-call(s32[8,128]{1,0:T(8,128)} %copy-done, bf16[1024,256]{1,0:T(8,128)(2,1)} %copy-done.23, ...), custom_call_target="tpu_custom_call" | custom-call | flops 7200000000 | bytes 1024 | tf_op jit(solution)/shard_map/self_forward_rest/pallas_call | solution.py:775
  37.2 18.1 %cross_forward.1 = (bf16[1024,256]{1,0:T(8,128)(2,1)}, bf16[1024,256]{1,0:T(8,128)(2,1)}, bf16[1024,256]{1,0:T(8,128)(2,1)}, bf16[1024,256]{1,0:T(8,128)(2,1)}, ...) custom-call(s32[8,128]{1,0:T(8,128)} %copy-done, ...), custom_call_target="tpu_custom_call" | custom-call | flops 12600000512 | bytes 1024 | tf_op jit(solution)/shard_map/cross_forward/pallas_call | solution.py:775
  55.4 4.8 %collective-permute-done.4.refs_6_.refs_8_ = bf16[1024,512]{1,0:T(8,128)(2,1)S(1)} collective-permute-done((bf16[1024,512]{1,0:T(8,128)(2,1)S(1)}, bf16[1024,512]{1,0:T(8,128)(2,1)S(1)}, u32[]{:S(2)}, u32[]{:S(2)}) %collective-permute-start.4) | collective-permute-done | bytes 1048608 | tf_op jit(solution)/shard_map/ppermute | solution.py:971
  60.1 2.7 %collective-permute-done.5.refs_7_.refs_9_ = bf16[1024,512]{1,0:T(8,128)(2,1)S(1)} collective-permute-done((bf16[1024,512]{1,0:T(8,128)(2,1)S(1)}, bf16[1024,512]{1,0:T(8,128)(2,1)S(1)}, u32[]{:S(2)}, u32[]{:S(2)}) %collective-permute-start.5) | collective-permute-done | bytes 1048608 | tf_op jit(solution)/shard_map/ppermute | solution.py:981
  63.8 16.0 %ffn_forward.1 = (bf16[1024,512]{1,0:T(8,128)(2,1)}, bf16[2048,512]{1,0:T(8,128)(2,1)}, bf16[1024,2048]{1,0:T(8,128)(2,1)}, bf16[1024,2048]{1,0:T(8,128)(2,1)}, f32[1024,512]{1,0:T(8,128)}, /*index=5*/f32[8,512]{1,0:T(8,128)}) custom-call(s32[8,128]{1,0:T(8,128)} %copy-done, bf16[512,1024]{1,0:T(8,128)(2,1)} %refs_1_.9, bf16[1024,512]{1,0:T(8,128)(2,1)} %refs_0_.9, ...), custom_call_target="tpu_custom_call" | custom-call | flops 10800000000 | bytes 1024 | tf_op jit(solution)/shard_map/ffn_forward/pallas_call | solution.py:775
  81.6 20.4 %ffn_backward.1 = (f32[1024,512]{1,0:T(8,128)}, bf16[256,4096]{1,0:T(8,128)(2,1)}, bf16[256,4096]{1,0:T(8,128)(2,1)}, f32[8,512]{1,0:T(8,128)}) custom-call(s32[8,128]{1,0:T(8,128)} %copy-done, bf16[1024,512]{1,0:T(8,128)(2,1)} %refs_0_.9, bf16[512,1024]{1,0:T(8,128)(2,1)} %refs_1_.9, f32[3,512]{1,0:T(4,128)} %refs_3_.14, f32[3,512]{1,0:T(4,128)} %refs_4_.11, ...), custom_call_target="tpu_custom_call" | custom-call | flops 16199999488 | bytes 1024 | tf_op jit(solution)/shard_map/ffn_backward/pallas_call | solution.py:775
  101.9 3.3 %collective-permute-done.6.refs_1_ = bf16[1024,512]{1,0:T(8,128)(2,1)S(1)} collective-permute-done((bf16[1024,512]{1,0:T(8,128)(2,1)}, bf16[1024,512]{1,0:T(8,128)(2,1)S(1)}, u32[]{:S(2)}, u32[]{:S(2)}) %collective-permute-start.6) | collective-permute-done | bytes 1048608 | tf_op jit(solution)/shard_map/ppermute | solution.py:991
  106.2 2.8 %fill_kernel.3 = bf16[2048,512]{1,0:T(8,128)(2,1)} custom-call(s32[8,128]{1,0:T(8,128)} %copy-done, bf16[2048,512]{1,0:T(8,128)(2,1)} %get-tuple-element.177.refs_0_, bf16[1024,512]{1,0:T(8,128)(2,1)} %copy-done.17), custom_call_target="tpu_custom_call", output_to_operand_aliasing={{}: (1, {})} | custom-call | flops 900000000 | bytes 1024 | tf_op jit(solution)/shard_map/fill_kernel/pallas_call | solution.py:775
  114.3 24.3 %cross_backward.1 = (f32[1024,512]{1,0:T(8,128)}, f32[2048,256]{1,0:T(8,128)}, bf16[1024,256]{1,0:T(8,128)(2,1)}, bf16[256,2048]{1,0:T(8,128)(2,1)}, bf16[256,2048]{1,0:T(8,128)(2,1)}, /*index=5*/f32[8,512]{1,0:T(8,128)}) custom-call(s32[8,128]{1,0:T(8,128)} %copy-done, bf16[1024,256]{1,0:T(8,128)(2,1)} %copy-done.26, bf16[1024,256]{1,0:T(8,128)(2,1)} %copy-done.27, ...), custom_call_target="tpu_custom_call" | custom-call | flops 19800000512 | bytes 1024 | tf_op jit(solution)/shard_map/cross_backward/pallas_call | solution.py:775
  143.2 3.0 %collective-permute-start.16 = (bf16[32,2048]{1,0:T(8,128)(2,1)S(1)}, bf16[32,2048]{1,0:T(8,128)(2,1)S(1)}, u32[]{:S(2)}, u32[]{:S(2)}) collective-permute-start(bf16[32,2048]{1,0:T(8,128)(2,1)S(1)} %get-tuple-element.311), channel_id=1, source_target_pairs={{0,16},{2,18},{4,20},{6,22},{8,24},{10,26},{12,28},{14,30},{16,0},... | collective-permute-start | bytes 393224 | tf_op jit(solution)/shard_map/ppermute | solution.py:929
  149.0 2.8 %collective-permute-start.12 = (bf16[4,32,1024]{2,1,0:T(8,128)(2,1)S(1)}, bf16[4,32,1024]{2,1,0:T(8,128)(2,1)S(1)}, u32[]{:S(2)}, u32[]{:S(2)}) collective-permute-start(bf16[4,32,1024]{2,1,0:T(8,128)(2,1)S(1)} %get-tuple-element.315), channel_id=1, source_target_pairs={{0,5},{1,4},{2,7},{3,6},{4,1},{5,0},{6,3},{7,2},{8,13},{9,12},{10,... | collective-permute-start | bytes 786440 | tf_op jit(solution)/shard_map/ppermute | solution.py:912
  152.3 3.8 %collective-permute-done.16 = bf16[32,2048]{1,0:T(8,128)(2,1)S(1)} collective-permute-done((bf16[32,2048]{1,0:T(8,128)(2,1)S(1)}, bf16[32,2048]{1,0:T(8,128)(2,1)S(1)}, u32[]{:S(2)}, u32[]{:S(2)}) %collective-permute-start.16) | collective-permute-done | bytes 131104 | tf_op jit(solution)/shard_map/ppermute | solution.py:929
  156.1 2.8 %collective-permute-start.14 = (bf16[4,32,1024]{2,1,0:T(8,128)(2,1)S(1)}, bf16[4,32,1024]{2,1,0:T(8,128)(2,1)S(1)}, u32[]{:S(2)}, u32[]{:S(2)}) collective-permute-start(bf16[4,32,1024]{2,1,0:T(8,128)(2,1)S(1)} %get-tuple-element.314), channel_id=1, source_target_pairs={{0,4},{2,6},{4,0},{6,2},{8,12},{10,14},{12,8},{14,10},{16,20},{18,... | collective-permute-start | bytes 786440 | tf_op jit(solution)/shard_map/ppermute | solution.py:914
  158.9 17.3 %self_backward.1 = (bf16[1024,256]{1,0:T(8,128)(2,1)}, bf16[1024,256]{1,0:T(8,128)(2,1)}, bf16[1024,256]{1,0:T(8,128)(2,1)}, bf16[1024,256]{1,0:T(8,128)(2,1)}, ...) custom-call(s32[8,128]{1,0:T(8,128)} %copy-done, ...), custom_call_target="tpu_custom_call" | custom-call | flops 14400000000 | bytes 1024 | tf_op jit(solution)/shard_map/self_backward/pallas_call | solution.py:775
  177.0 3.4 %collective-permute-start.20 = (bf16[32,1024]{1,0:T(8,128)(2,1)S(1)}, bf16[32,1024]{1,0:T(8,128)(2,1)S(1)}, u32[]{:S(2)}, u32[]{:S(2)}) collective-permute-start(bf16[32,1024]{1,0:T(8,128)(2,1)S(1)} %get-tuple-element.324), channel_id=1, source_target_pairs={{0,16},{2,18},{4,20},{6,22},{8,24},{10,26},{12,28},{14,30},{16,0},... | collective-permute-start | bytes 196616 | tf_op jit(solution)/shard_map/ppermute | solution.py:929
  180.5 6.1 %input_backward.1 = (f32[2048,256]{1,0:T(8,128)}, bf16[1024,256]{1,0:T(8,128)(2,1)}) custom-call(s32[8,128]{1,0:T(8,128)} %copy-done, bf16[1024,256]{1,0:T(8,128)(2,1)} %copy-done.23, bf16[1024,256]{1,0:T(8,128)(2,1)} %copy-done.24, bf16[512,256]{1,0:T(8,128)(2,1)} %refs_2_.19, bf16[512,256]{1,0:T(8,128)(2,1)} %refs_3_.15, bf16[512,256]{1,0:T(8,128)(2,1)} %refs_4_.13, ...), custom_call_target="tpu_custom_call" | custom-call | flops 4499999744 | bytes 1024 | tf_op jit(solution)/shard_map/input_backward/pallas_call | solution.py:775
  192.2 2.6 %fill_kernel.5 = f32[2048,256]{1,0:T(8,128)} custom-call(s32[8,128]{1,0:T(8,128)} %copy-done, f32[2048,256]{1,0:T(8,128)} %get-tuple-element.254.refs_0_, bf16[1024,256]{1,0:T(8,128)(2,1)} %copy-done.19), custom_call_target="tpu_custom_call", output_to_operand_aliasing={{}: (1, {})} | custom-call | flops 900000000 | bytes 1024 | tf_op jit(solution)/shard_map/fill_kernel/pallas_call | solution.py:775
  194.9 4.5 %collective-permute-done.24 = bf16[4,32,1152]{2,1,0:T(8,128)(2,1)S(1)} collective-permute-done((bf16[4,32,1152]{2,1,0:T(8,128)(2,1)S(1)}, bf16[4,32,1152]{2,1,0:T(8,128)(2,1)S(1)}, u32[]{:S(2)}, u32[]{:S(2)}) %collective-permute-start.24) | collective-permute-done | bytes 294944 | tf_op jit(solution)/shard_map/ppermute | solution.py:912
  199.4 4.6 %collective-permute-done.26 = bf16[4,32,1152]{2,1,0:T(8,128)(2,1)S(1)} collective-permute-done((bf16[4,32,1152]{2,1,0:T(8,128)(2,1)S(1)}, bf16[4,32,1152]{2,1,0:T(8,128)(2,1)S(1)}, u32[]{:S(2)}, u32[]{:S(2)}) %collective-permute-start.26) | collective-permute-done | bytes 294944 | tf_op jit(solution)/shard_map/ppermute | solution.py:914
  206.7 2.8 %collective-permute-start.29 = (bf16[32,1152]{1,0:T(8,128)(2,1)S(1)}, bf16[32,1152]{1,0:T(8,128)(2,1)S(1)}, u32[]{:S(2)}, u32[]{:S(2)}) collective-permute-start(bf16[32,1152]{1,0:T(8,128)(2,1)S(1)} %get-tuple-element.319), channel_id=1, source_target_pairs={{0,24},{2,26},{4,28},{6,30},{8,0},{10,2},{12,4},{14,6},{16,8},{18,... | collective-permute-start | bytes 221192 | tf_op jit(solution)/shard_map/ppermute | solution.py:929
  216.8 6.5 %collective-permute-done.23.refs_1_ = bf16[1024,256]{1,0:T(8,128)(2,1)S(1)} collective-permute-done((bf16[1024,256]{1,0:T(8,128)(2,1)S(1)}, bf16[1024,256]{1,0:T(8,128)(2,1)S(1)}, u32[]{:S(2)}, u32[]{:S(2)}) %collective-permute-start.23) | collective-permute-done | bytes 524320 | tf_op jit(solution)/shard_map/ppermute | solution.py:1062
  224.0 2.6 %fill_kernel.4 = f32[2048,256]{1,0:T(8,128)} custom-call(s32[8,128]{1,0:T(8,128)} %copy-done, f32[2048,256]{1,0:T(8,128)} %get-tuple-element.252.refs_0_, bf16[1024,256]{1,0:T(8,128)(2,1)} %copy-done.20), custom_call_target="tpu_custom_call", output_to_operand_aliasing={{}: (1, {})} | custom-call | flops 900000000 | bytes 1024 | tf_op jit(solution)/shard_map/fill_kernel/pallas_call | solution.py:775
  (143 shorter events, 49.2 us)
Async XLA Ops:
  5.2 15.0 %collective-permute-start = (bf16[1024,256]{1,0:T(8,128)(2,1)S(1)}, bf16[1024,256]{1,0:T(8,128)(2,1)S(1)}, u32[]{:S(2)}, u32[]{:S(2)}) collective-permute-start(bf16[1024,256]{1,0:T(8,128)(2,1)S(1)} %pack_weights.3), channel_id=1, source_target_pairs={{0,1},{1,0},{2,3},{3,2},{4,5},{5,4},{6,7},{7,6},{8,9},{9,8},{10,11... | collective-permute-start | bytes 1572872 | tf_op jit(solution)/shard_map/ppermute | solution.py:881
  20.2 14.3 %collective-permute-start.2 = (bf16[1024,256]{1,0:T(8,128)(2,1)S(1)}, bf16[1024,256]{1,0:T(8,128)(2,1)S(1)}, u32[]{:S(2)}, u32[]{:S(2)}) collective-permute-start(bf16[1024,256]{1,0:T(8,128)(2,1)S(1)} %get-tuple-element.158), channel_id=1, source_target_pairs={{0,1},{1,0},{2,3},{3,2},{4,5},{5,4},{6,7},{7,6},{8,9},{9,8},{10,11... | collective-permute-start | bytes 1572872 | tf_op jit(solution)/shard_map/ppermute | solution.py:962
  34.5 25.6 %collective-permute-start.4 = (bf16[1024,512]{1,0:T(8,128)(2,1)S(1)}, bf16[1024,512]{1,0:T(8,128)(2,1)S(1)}, u32[]{:S(2)}, u32[]{:S(2)}) collective-permute-start(bf16[1024,512]{1,0:T(8,128)(2,1)S(1)} %get-tuple-element.174), channel_id=1, source_target_pairs={{0,1},{1,0},{2,3},{3,2},{4,5},{5,4},{6,7},{7,6},{8,9},{9,8},{10,11... | collective-permute-start | bytes 3145736 | tf_op jit(solution)/shard_map/ppermute | solution.py:971
  79.8 25.5 %collective-permute-start.6 = (bf16[1024,512]{1,0:T(8,128)(2,1)}, bf16[1024,512]{1,0:T(8,128)(2,1)S(1)}, u32[]{:S(2)}, u32[]{:S(2)}) collective-permute-start(bf16[1024,512]{1,0:T(8,128)(2,1)} %get-tuple-element.186), channel_id=1, source_target_pairs={{0,1},{1,0},{2,3},{3,2},{4,5},{5,4},{6,7},{7,6},{8,9},{9,8},{10,11... | collective-permute-start | bytes 3145736 | tf_op jit(solution)/shard_map/ppermute | solution.py:991
  110.6 28.0 %collective-permute-start.10 = (bf16[4,32,2048]{2,1,0:T(8,128)(2,1)S(1)}, bf16[4,32,2048]{2,1,0:T(8,128)(2,1)S(1)}, u32[]{:S(2)}, u32[]{:S(2)}) collective-permute-start(bf16[4,32,2048]{2,1,0:T(8,128)(2,1)S(1)} %get-tuple-element.304), channel_id=1, source_target_pairs={{0,4},{2,6},{4,0},{6,2},{8,12},{10,14},{12,8},{14,10},{16,20},{18,... | collective-permute-start | bytes 1572872 | tf_op jit(solution)/shard_map/ppermute | solution.py:914
  112.4 26.3 %collective-permute-start.8 = (bf16[4,32,2048]{2,1,0:T(8,128)(2,1)S(1)}, bf16[4,32,2048]{2,1,0:T(8,128)(2,1)S(1)}, u32[]{:S(2)}, u32[]{:S(2)}) collective-permute-start(bf16[4,32,2048]{2,1,0:T(8,128)(2,1)S(1)} %get-tuple-element.305), channel_id=1, source_target_pairs={{0,5},{1,4},{2,7},{3,6},{4,1},{5,0},{6,3},{7,2},{8,13},{9,12},{10,... | collective-permute-start | bytes 1572872 | tf_op jit(solution)/shard_map/ppermute | solution.py:912
  114.0 24.8 %collective-permute-start.9 = (bf16[4,32,2048]{2,1,0:T(8,128)(2,1)S(1)}, bf16[4,32,2048]{2,1,0:T(8,128)(2,1)}, u32[]{:S(2)}, u32[]{:S(2)}) collective-permute-start(bf16[4,32,2048]{2,1,0:T(8,128)(2,1)S(1)} %get-tuple-element.306), channel_id=1, source_target_pairs={{0,1},{1,0},{2,3},{3,2},{4,5},{5,4},{6,7},{7,6},{8,9},{9,8},{10,11... | collective-permute-start | bytes 1572872 | tf_op jit(solution)/shard_map/ppermute | solution.py:913
  139.5 9.0 %collective-permute-start.11 = (bf16[256,2048]{1,0:T(8,128)(2,1)}, bf16[256,2048]{1,0:T(8,128)(2,1)S(1)}, u32[]{:S(2)}, u32[]{:S(2)}) collective-permute-start(bf16[256,2048]{1,0:T(8,128)(2,1)} %get-tuple-element.211), channel_id=1, source_target_pairs={{0,2},{2,0},{4,6},{6,4},{8,10},{10,8},{12,14},{14,12},{16,18},{18,... | collective-permute-start | bytes 3145736 | tf_op jit(solution)/shard_map/ppermute | solution.py:899
  143.1 8.7 %collective-permute-start.15 = (bf16[32,2048]{1,0:T(8,128)(2,1)S(1)}, bf16[32,2048]{1,0:T(8,128)(2,1)S(1)}, u32[]{:S(2)}, u32[]{:S(2)}) collective-permute-start(bf16[32,2048]{1,0:T(8,128)(2,1)S(1)} %get-tuple-element.312), channel_id=1, source_target_pairs={{0,8},{2,10},{4,12},{6,14},{8,16},{10,18},{12,20},{14,22},{16,24},... | collective-permute-start | bytes 393224 | tf_op jit(solution)/shard_map/ppermute | solution.py:929
  143.2 12.9 %collective-permute-start.16 = (bf16[32,2048]{1,0:T(8,128)(2,1)S(1)}, bf16[32,2048]{1,0:T(8,128)(2,1)S(1)}, u32[]{:S(2)}, u32[]{:S(2)}) collective-permute-start(bf16[32,2048]{1,0:T(8,128)(2,1)S(1)} %get-tuple-element.311), channel_id=1, source_target_pairs={{0,16},{2,18},{4,20},{6,22},{8,24},{10,26},{12,28},{14,30},{16,0},... | collective-permute-start | bytes 393224 | tf_op jit(solution)/shard_map/ppermute | solution.py:929
  146.2 30.1 %collective-permute-start.17 = (bf16[32,2048]{1,0:T(8,128)(2,1)S(1)}, bf16[32,2048]{1,0:T(8,128)(2,1)S(1)}, u32[]{:S(2)}, u32[]{:S(2)}) collective-permute-start(bf16[32,2048]{1,0:T(8,128)(2,1)S(1)} %get-tuple-element.310), channel_id=1, source_target_pairs={{0,24},{2,26},{4,28},{6,30},{8,0},{10,2},{12,4},{14,6},{16,8},{18,... | collective-permute-start | bytes 393224 | tf_op jit(solution)/shard_map/ppermute | solution.py:929
  147.0 29.3 %collective-permute-start.18 = (bf16[1024,256]{1,0:T(8,128)(2,1)S(1)}, bf16[1024,256]{1,0:T(8,128)(2,1)S(1)}, u32[]{:S(2)}, u32[]{:S(2)}) collective-permute-start(bf16[1024,256]{1,0:T(8,128)(2,1)S(1)} %copy-done.25), channel_id=1, source_target_pairs={{0,1},{1,0},{2,3},{3,2},{4,5},{5,4},{6,7},{7,6},{8,9},{9,8},{10,11... | collective-permute-start | bytes 1572872 | tf_op jit(solution)/shard_map/ppermute | solution.py:1030
  149.0 27.3 %collective-permute-start.12 = (bf16[4,32,1024]{2,1,0:T(8,128)(2,1)S(1)}, bf16[4,32,1024]{2,1,0:T(8,128)(2,1)S(1)}, u32[]{:S(2)}, u32[]{:S(2)}) collective-permute-start(bf16[4,32,1024]{2,1,0:T(8,128)(2,1)S(1)} %get-tuple-element.315), channel_id=1, source_target_pairs={{0,5},{1,4},{2,7},{3,6},{4,1},{5,0},{6,3},{7,2},{8,13},{9,12},{10,... | collective-permute-start | bytes 786440 | tf_op jit(solution)/shard_map/ppermute | solution.py:912
  151.9 24.5 %collective-permute-start.13 = (bf16[4,32,1024]{2,1,0:T(8,128)(2,1)S(1)}, bf16[4,32,1024]{2,1,0:T(8,128)(2,1)S(1)}, u32[]{:S(2)}, u32[]{:S(2)}) collective-permute-start(bf16[4,32,1024]{2,1,0:T(8,128)(2,1)S(1)} %get-tuple-element.316), channel_id=1, source_target_pairs={{0,1},{1,0},{2,3},{3,2},{4,5},{5,4},{6,7},{7,6},{8,9},{9,8},{10,11... | collective-permute-start | bytes 786440 | tf_op jit(solution)/shard_map/ppermute | solution.py:913
  156.1 20.3 %collective-permute-start.14 = (bf16[4,32,1024]{2,1,0:T(8,128)(2,1)S(1)}, bf16[4,32,1024]{2,1,0:T(8,128)(2,1)S(1)}, u32[]{:S(2)}, u32[]{:S(2)}) collective-permute-start(bf16[4,32,1024]{2,1,0:T(8,128)(2,1)S(1)} %get-tuple-element.314), channel_id=1, source_target_pairs={{0,4},{2,6},{4,0},{6,2},{8,12},{10,14},{12,8},{14,10},{16,20},{18,... | collective-permute-start | bytes 786440 | tf_op jit(solution)/shard_map/ppermute | solution.py:914
  176.4 11.1 %collective-permute-start.22 = (bf16[256,2304]{1,0:T(8,128)(2,1)}, bf16[256,2304]{1,0:T(8,128)(2,1)S(1)}, u32[]{:S(2)}, u32[]{:S(2)}) collective-permute-start(bf16[256,2304]{1,0:T(8,128)(2,1)} %get-tuple-element.251), channel_id=1, source_target_pairs={{0,2},{2,0},{4,6},{6,4},{8,10},{10,8},{12,14},{14,12},{16,18},{18,... | collective-permute-start | bytes 3538952 | tf_op jit(solution)/shard_map/ppermute | solution.py:899
  176.6 10.8 %collective-permute-start.19 = (bf16[32,1024]{1,0:T(8,128)(2,1)S(1)}, bf16[32,1024]{1,0:T(8,128)(2,1)S(1)}, u32[]{:S(2)}, u32[]{:S(2)}) collective-permute-start(bf16[32,1024]{1,0:T(8,128)(2,1)S(1)} %get-tuple-element.325), channel_id=1, source_target_pairs={{0,8},{2,10},{4,12},{6,14},{8,16},{10,18},{12,20},{14,22},{16,24},... | collective-permute-start | bytes 196616 | tf_op jit(solution)/shard_map/ppermute | solution.py:929
  177.0 10.5 %collective-permute-start.20 = (bf16[32,1024]{1,0:T(8,128)(2,1)S(1)}, bf16[32,1024]{1,0:T(8,128)(2,1)S(1)}, u32[]{:S(2)}, u32[]{:S(2)}) collective-permute-start(bf16[32,1024]{1,0:T(8,128)(2,1)S(1)} %get-tuple-element.324), channel_id=1, source_target_pairs={{0,16},{2,18},{4,20},{6,22},{8,24},{10,26},{12,28},{14,30},{16,0},... | collective-permute-start | bytes 196616 | tf_op jit(solution)/shard_map/ppermute | solution.py:929
  188.5 10.9 %collective-permute-start.24 = (bf16[4,32,1152]{2,1,0:T(8,128)(2,1)S(1)}, bf16[4,32,1152]{2,1,0:T(8,128)(2,1)S(1)}, u32[]{:S(2)}, u32[]{:S(2)}) collective-permute-start(bf16[4,32,1152]{2,1,0:T(8,128)(2,1)S(1)} %get-tuple-element.308), channel_id=1, source_target_pairs={{0,5},{1,4},{2,7},{3,6},{4,1},{5,0},{6,3},{7,2},{8,13},{9,12},{10,... | collective-permute-start | bytes 884744 | tf_op jit(solution)/shard_map/ppermute | solution.py:912
  188.8 15.2 %collective-permute-start.26 = (bf16[4,32,1152]{2,1,0:T(8,128)(2,1)S(1)}, bf16[4,32,1152]{2,1,0:T(8,128)(2,1)S(1)}, u32[]{:S(2)}, u32[]{:S(2)}) collective-permute-start(bf16[4,32,1152]{2,1,0:T(8,128)(2,1)S(1)} %get-tuple-element.309), channel_id=1, source_target_pairs={{0,4},{2,6},{4,0},{6,2},{8,12},{10,14},{12,8},{14,10},{16,20},{18,... | collective-permute-start | bytes 884744 | tf_op jit(solution)/shard_map/ppermute | solution.py:914
  191.3 13.3 %collective-permute-start.25 = (bf16[4,32,1152]{2,1,0:T(8,128)(2,1)S(1)}, bf16[4,32,1152]{2,1,0:T(8,128)(2,1)S(1)}, u32[]{:S(2)}, u32[]{:S(2)}) collective-permute-start(bf16[4,32,1152]{2,1,0:T(8,128)(2,1)S(1)} %slice.136), channel_id=1, source_target_pairs={{0,1},{1,0},{2,3},{3,2},{4,5},{5,4},{6,7},{7,6},{8,9},{9,8},{10,11... | collective-permute-start | bytes 884744 | tf_op jit(solution)/shard_map/ppermute | solution.py:913
  206.4 7.7 %collective-permute-start.28 = (bf16[32,1152]{1,0:T(8,128)(2,1)S(1)}, bf16[32,1152]{1,0:T(8,128)(2,1)S(1)}, u32[]{:S(2)}, u32[]{:S(2)}) collective-permute-start(bf16[32,1152]{1,0:T(8,128)(2,1)S(1)} %get-tuple-element.320), channel_id=1, source_target_pairs={{0,16},{2,18},{4,20},{6,22},{8,24},{10,26},{12,28},{14,30},{16,0},... | collective-permute-start | bytes 221192 | tf_op jit(solution)/shard_map/ppermute | solution.py:929
  206.7 7.4 %collective-permute-start.29 = (bf16[32,1152]{1,0:T(8,128)(2,1)S(1)}, bf16[32,1152]{1,0:T(8,128)(2,1)S(1)}, u32[]{:S(2)}, u32[]{:S(2)}) collective-permute-start(bf16[32,1152]{1,0:T(8,128)(2,1)S(1)} %get-tuple-element.319), channel_id=1, source_target_pairs={{0,24},{2,26},{4,28},{6,30},{8,0},{10,2},{12,4},{14,6},{16,8},{18,... | collective-permute-start | bytes 221192 | tf_op jit(solution)/shard_map/ppermute | solution.py:929
  210.2 13.0 %collective-permute-start.23 = (bf16[1024,256]{1,0:T(8,128)(2,1)S(1)}, bf16[1024,256]{1,0:T(8,128)(2,1)S(1)}, u32[]{:S(2)}, u32[]{:S(2)}) collective-permute-start(bf16[1024,256]{1,0:T(8,128)(2,1)S(1)} %copy-done.28), channel_id=1, source_target_pairs={{0,1},{1,0},{2,3},{3,2},{4,5},{5,4},{6,7},{7,6},{8,9},{9,8},{10,11... | collective-permute-start | bytes 1572872 | tf_op jit(solution)/shard_map/ppermute | solution.py:1062
  (35 other events, 140.6 us)
